TPU v7x, 128 devices: a whole 4x4x4 slice. The times are simulated.
128 devices in a mesh: row: 8 (over x, z_hi), col: 16 (over y, z_lo, core).
Axes of the slice: x: 4, y: 4, z: 4 (z_hi: 2, z_lo: 2; z = z_hi * 2 + z_lo), core: 2. Of those that a mesh axis runs over, the one named last changes fastest.
Arguments:
- a_blocks: bfloat16 [8, 16, 4, 7, 128, 128], P('row', 'col'), may hold values from -6 to 6
- a_rows: int32 [8, 16, 4, 7], P('row', 'col'), may hold values from 0 to 7, as said below
- b_blocks: bfloat16 [8, 16, 2, 4, 3, 128, 128], P('row', 'col'), may hold values from -0.09375 to 0.09375
- b_cols: int32 [8, 16, 2, 4, 3], P('row', 'col'), may hold values from 0 to 3, as said below
- screen: int32 [8, 16, 16, 4, 7, 3], P('row', 'col'), may hold values 0 or 1
- keep: int32 [8, 16, 32], P('row', 'col'), may hold values 0 or 1
- owners: int32 [8, 16, 32, 1], P('row', 'col'), may hold values from 0 to 15; in each aligned block of 32 rows (0 to 31, 32 to 63, ..., all dimensions but the last counted through in order) at most 2 rows name the same one
Outputs:
- owned: bfloat16 [8, 16, 16, 2, 128, 128], P('row', 'col')
Inputs may be any that keep to these rules, and one draw needn't show every extreme that they name: `a_rows`: for each device and block column k, the 7 entries are distinct block rows. `b_cols`: for each device, tile and block row k, the 3 entries are distinct block columns. `owners`: among the blocks of one device at most 2 have the same owner.
All inputs are finite; a program needn't handle non-finite values. No bound on the sum of `screen` or of `keep` on one device may be relied on, other than what follows from the above.
Results may differ from a plain program's by a relative error of at most 0.001.
Values may be sent and summed in bfloat16 or wider, within the bound.
A program may use at most 128 MiB of HBM per device.

v0:
```python
import jax
import jax.numpy as jnp
from jax import lax
from jax.sharding import PartitionSpec as P


def passed_along(block, axis, distance):
    devices = range(lax.axis_size(axis))
    route = [((i - distance) % len(devices), i) for i in devices]
    return lax.ppermute(block, axis, route)


def tile_product(a_data, a_list, b_data, b_list, screen_now, rows_count, cols_count):
    row_hot = (a_list[:, :, None] == jnp.arange(rows_count, dtype=jnp.int32)).astype(jnp.bfloat16)
    col_hot = (b_list[:, :, None] == jnp.arange(cols_count, dtype=jnp.int32)).astype(jnp.bfloat16)
    combo = (
        jnp.einsum("kar,kbc->kabrc", row_hot, col_hot)
        * screen_now.astype(jnp.bfloat16)[:, :, :, None, None]
    )
    a_chosen = jnp.einsum(
        "kabrc,kaxy->kcrxy", combo, a_data, preferred_element_type=jnp.float32
    ).astype(jnp.bfloat16)
    b_chosen = jnp.einsum(
        "kbc,kbyz->kcyz", col_hot, b_data, preferred_element_type=jnp.float32
    ).astype(jnp.bfloat16)
    return jnp.einsum("kcrxy,kcyz->rcxz", a_chosen, b_chosen, preferred_element_type=jnp.float32)


def on_device(a_blocks, a_rows, b_blocks, b_cols, screen, keep, owners):
    grid_rows = lax.axis_size("row")
    grid_cols = lax.axis_size("col")
    my_row = lax.axis_index("row")
    inner = a_blocks.shape[2]
    rows_tile = 2 * inner
    width = a_blocks.shape[-1]
    slot_count = max(2, (2 * inner * inner + grid_cols - 1) // grid_cols)
    start_total = jnp.zeros((rows_tile, inner, width, width), jnp.float32)

    def advance(s, carry):
        a_data, a_list, b_pair, b_lists, total = carry
        total = total + tile_product(
            a_data, a_list, b_pair[0], b_lists[0], screen[0, 0, s], rows_tile, inner
        )
        a_data, a_list = passed_along((a_data, a_list), "col", -1)
        b_pair, b_lists = passed_along((b_pair, b_lists), "row", -1)
        last_row = my_row == grid_rows - 1
        b_pair = jnp.where(last_row, b_pair[::-1], b_pair)
        b_lists = jnp.where(last_row, b_lists[::-1], b_lists)
        return (a_data, a_list, b_pair, b_lists, total)

    carry = (a_blocks[0, 0], a_rows[0, 0], b_blocks[0, 0], b_cols[0, 0], start_total)
    a_data, a_list, b_pair, b_lists, total = lax.fori_loop(0, grid_cols - 1, advance, carry)
    total = total + tile_product(
        a_data, a_list, b_pair[0], b_lists[0], screen[0, 0, grid_cols - 1], rows_tile, inner
    )
    tile = total.astype(jnp.bfloat16).reshape(rows_tile * inner, width, width)
    owner_row = owners[0, 0, :, 0]
    count = owner_row.shape[0]
    order = jnp.arange(count, dtype=jnp.int32)
    same = (owner_row[:, None] == owner_row[None, :]) & (order[None, :] < order[:, None])
    rank = jnp.sum(same.astype(jnp.int32), axis=1)
    dest_hot = owner_row[:, None] == jnp.arange(grid_cols, dtype=jnp.int32)
    slot_hot = rank[:, None] == jnp.arange(slot_count, dtype=jnp.int32)
    table = dest_hot[:, :, None] & slot_hot[:, None, :] & (keep[0, 0][:, None, None] == 1)
    outgoing = jnp.einsum(
        "mos,mxz->osxz", table.astype(jnp.bfloat16), tile, preferred_element_type=jnp.float32
    ).astype(jnp.bfloat16)
    return lax.all_to_all(outgoing[None, None], "col", split_axis=2, concat_axis=2, tiled=True)


def solution(mesh):
    in_specs = (
        P("row", "col", None, None, None, None),
        P("row", "col", None, None),
        P("row", "col", None, None, None, None, None),
        P("row", "col", None, None, None),
        P("row", "col", None, None, None, None),
        P("row", "col", None),
        P("row", "col", None, None),
    )
    out_specs = P("row", "col", None, None, None, None)
    return jax.shard_map(
        on_device, mesh=mesh, in_specs=in_specs, out_specs=out_specs, check_vma=False
    )
```

profile of v0, /device:TPU:1, one launch (start us, length us, event | category | flops | bytes accessed | tf_op | source)
XLA Modules:
  0.0 584.2 jit_solution(419123033151540090)
XLA Ops:
  3.7 549.2 %while.24 = (s32[]{:T(128)}, bf16[4,7,128,128]{3,2,1,0:T(8,128)(2,1)}, s32[4,7]{1,0:T(4,128)S(1)}, bf16[2,4,3,128,128]{4,3,2,1,0:T(8,128)(2,1)}, s32[2,4,3]{2,1,...) while((s32[]{:T(128)}, ...), condition=%wide.region_3.4_spmd.clone, body=%wide.region_1.3_spmd.clone.sunk | while | flops 569531840 | bytes 30025216 | solution.py:52
  3.7 6.6 %collective-permute-start.2 = (bf16[2,4,3,128,128]{4,3,2,1,0:T(8,128)(2,1)}, bf16[2,4,3,128,128]{4,3,2,1,0:T(8,128)(2,1)}, u32[]{:S(2)}, u32[]{:S(2)}) collective-permute-start(bf16[2,4,3,128,128]{4,3,2,1,0:T(8,128)(2,1)} %get-tuple-element.350), channel_id=1, source_target_pairs={{16,0},{32,16},{48,32},{64,48},{80,64},{96,80},{112,96},{0,112},{1... | collective-permute-start | bytes 2359304 | tf_op jit(solution)/shard_map/while/body/eval_jaxpr/ppermute | solution.py:10
  12.6 2.8 collective-permute-start.1
  15.5 2.8 copy.139
  22.5 13.2 %collective-permute-done.3 = s32[2,4,3]{2,1,0:T(4,128)S(1)} collective-permute-done((s32[2,4,3]{2,1,0:T(4,128)S(1)}, s32[2,4,3]{2,1,0:T(4,128)S(1)}, u32[]{:S(2)}, u32[]{:S(2)}) %collective-permute-start.3) | collective-permute-done | bytes 128 | tf_op jit(solution)/shard_map/while/body/eval_jaxpr/ppermute | solution.py:10
  35.7 2.5 reverse_select_fusion.4
  38.3 8.4 %collective-permute-done.1 = s32[4,7]{1,0:T(4,128)S(1)} collective-permute-done((s32[4,7]{1,0:T(4,128)S(1)}, s32[4,7]{1,0:T(4,128)S(1)}, u32[]{:S(2)}, u32[]{:S(2)}) %collective-permute-start.1) | collective-permute-done | bytes 144 | tf_op jit(solution)/shard_map/while/body/eval_jaxpr/ppermute | solution.py:10
  46.7 6.4 %collective-permute-start.3 = (s32[2,4,3]{2,1,0:T(4,128)S(1)}, s32[2,4,3]{2,1,0:T(4,128)S(1)}, u32[]{:S(2)}, u32[]{:S(2)}) collective-permute-start(s32[2,4,3]{2,1,0:T(4,128)S(1)} %get-tuple-element.351), channel_id=1, source_target_pairs={{16,0},{32,16},{48,32},{64,48},{80,64},{96,80},{112,96},{0,112},{1... | collective-permute-start | bytes 296 | tf_op jit(solution)/shard_map/while/body/eval_jaxpr/ppermute | solution.py:10
  54.3 2.8 copy.139
  61.3 11.9 %collective-permute-done.3 = s32[2,4,3]{2,1,0:T(4,128)S(1)} collective-permute-done((s32[2,4,3]{2,1,0:T(4,128)S(1)}, s32[2,4,3]{2,1,0:T(4,128)S(1)}, u32[]{:S(2)}, u32[]{:S(2)}) %collective-permute-start.3) | collective-permute-done | bytes 128 | tf_op jit(solution)/shard_map/while/body/eval_jaxpr/ppermute | solution.py:10
  73.2 2.5 reverse_select_fusion.4
  75.8 16.8 %collective-permute-done.1 = s32[4,7]{1,0:T(4,128)S(1)} collective-permute-done((s32[4,7]{1,0:T(4,128)S(1)}, s32[4,7]{1,0:T(4,128)S(1)}, u32[]{:S(2)}, u32[]{:S(2)}) %collective-permute-start.1) | collective-permute-done | bytes 144 | tf_op jit(solution)/shard_map/while/body/eval_jaxpr/ppermute | solution.py:10
  93.8 2.8 copy.139
  100.8 8.0 %collective-permute-done.3 = s32[2,4,3]{2,1,0:T(4,128)S(1)} collective-permute-done((s32[2,4,3]{2,1,0:T(4,128)S(1)}, s32[2,4,3]{2,1,0:T(4,128)S(1)}, u32[]{:S(2)}, u32[]{:S(2)}) %collective-permute-start.3) | collective-permute-done | bytes 128 | tf_op jit(solution)/shard_map/while/body/eval_jaxpr/ppermute | solution.py:10
  108.8 2.5 reverse_select_fusion.4
  111.4 3.3 collective-permute-start.2
  114.7 19.4 %collective-permute-start.3 = (s32[2,4,3]{2,1,0:T(4,128)S(1)}, s32[2,4,3]{2,1,0:T(4,128)S(1)}, u32[]{:S(2)}, u32[]{:S(2)}) collective-permute-start(s32[2,4,3]{2,1,0:T(4,128)S(1)} %get-tuple-element.351), channel_id=1, source_target_pairs={{16,0},{32,16},{48,32},{64,48},{80,64},{96,80},{112,96},{0,112},{1... | collective-permute-start | bytes 296 | tf_op jit(solution)/shard_map/while/body/eval_jaxpr/ppermute | solution.py:10
  135.4 2.8 copy.139
  142.5 2.5 reverse_select_fusion.4
  145.0 20.1 %collective-permute-done.1 = s32[4,7]{1,0:T(4,128)S(1)} collective-permute-done((s32[4,7]{1,0:T(4,128)S(1)}, s32[4,7]{1,0:T(4,128)S(1)}, u32[]{:S(2)}, u32[]{:S(2)}) %collective-permute-start.1) | collective-permute-done | bytes 144 | tf_op jit(solution)/shard_map/while/body/eval_jaxpr/ppermute | solution.py:10
  166.4 2.8 copy.139
  173.4 7.8 %collective-permute-done.3 = s32[2,4,3]{2,1,0:T(4,128)S(1)} collective-permute-done((s32[2,4,3]{2,1,0:T(4,128)S(1)}, s32[2,4,3]{2,1,0:T(4,128)S(1)}, u32[]{:S(2)}, u32[]{:S(2)}) %collective-permute-start.3) | collective-permute-done | bytes 128 | tf_op jit(solution)/shard_map/while/body/eval_jaxpr/ppermute | solution.py:10
  181.3 2.5 reverse_select_fusion.4
  183.8 22.9 %collective-permute-start.3 = (s32[2,4,3]{2,1,0:T(4,128)S(1)}, s32[2,4,3]{2,1,0:T(4,128)S(1)}, u32[]{:S(2)}, u32[]{:S(2)}) collective-permute-start(s32[2,4,3]{2,1,0:T(4,128)S(1)} %get-tuple-element.351), channel_id=1, source_target_pairs={{16,0},{32,16},{48,32},{64,48},{80,64},{96,80},{112,96},{0,112},{1... | collective-permute-start | bytes 296 | tf_op jit(solution)/shard_map/while/body/eval_jaxpr/ppermute | solution.py:10
  208.0 2.8 copy.139
  215.1 2.5 reverse_select_fusion.4
  217.6 23.1 %collective-permute-done.1 = s32[4,7]{1,0:T(4,128)S(1)} collective-permute-done((s32[4,7]{1,0:T(4,128)S(1)}, s32[4,7]{1,0:T(4,128)S(1)}, u32[]{:S(2)}, u32[]{:S(2)}) %collective-permute-start.1) | collective-permute-done | bytes 144 | tf_op jit(solution)/shard_map/while/body/eval_jaxpr/ppermute | solution.py:10
  242.0 2.8 copy.139
  249.0 7.8 %collective-permute-done.3 = s32[2,4,3]{2,1,0:T(4,128)S(1)} collective-permute-done((s32[2,4,3]{2,1,0:T(4,128)S(1)}, s32[2,4,3]{2,1,0:T(4,128)S(1)}, u32[]{:S(2)}, u32[]{:S(2)}) %collective-permute-start.3) | collective-permute-done | bytes 128 | tf_op jit(solution)/shard_map/while/body/eval_jaxpr/ppermute | solution.py:10
  256.9 2.5 reverse_select_fusion.4
  259.4 3.0 collective-permute-start.2
  262.4 19.9 %collective-permute-start.3 = (s32[2,4,3]{2,1,0:T(4,128)S(1)}, s32[2,4,3]{2,1,0:T(4,128)S(1)}, u32[]{:S(2)}, u32[]{:S(2)}) collective-permute-start(s32[2,4,3]{2,1,0:T(4,128)S(1)} %get-tuple-element.351), channel_id=1, source_target_pairs={{16,0},{32,16},{48,32},{64,48},{80,64},{96,80},{112,96},{0,112},{1... | collective-permute-start | bytes 296 | tf_op jit(solution)/shard_map/while/body/eval_jaxpr/ppermute | solution.py:10
  283.6 2.8 copy.139
  290.6 2.5 reverse_select_fusion.4
  293.2 20.4 %collective-permute-done.1 = s32[4,7]{1,0:T(4,128)S(1)} collective-permute-done((s32[4,7]{1,0:T(4,128)S(1)}, s32[4,7]{1,0:T(4,128)S(1)}, u32[]{:S(2)}, u32[]{:S(2)}) %collective-permute-start.1) | collective-permute-done | bytes 144 | tf_op jit(solution)/shard_map/while/body/eval_jaxpr/ppermute | solution.py:10
  314.9 2.8 copy.139
  321.9 7.8 %collective-permute-done.3 = s32[2,4,3]{2,1,0:T(4,128)S(1)} collective-permute-done((s32[2,4,3]{2,1,0:T(4,128)S(1)}, s32[2,4,3]{2,1,0:T(4,128)S(1)}, u32[]{:S(2)}, u32[]{:S(2)}) %collective-permute-start.3) | collective-permute-done | bytes 128 | tf_op jit(solution)/shard_map/while/body/eval_jaxpr/ppermute | solution.py:10
  329.8 2.5 reverse_select_fusion.4
  332.3 3.0 collective-permute-start.2
  335.3 19.9 %collective-permute-start.3 = (s32[2,4,3]{2,1,0:T(4,128)S(1)}, s32[2,4,3]{2,1,0:T(4,128)S(1)}, u32[]{:S(2)}, u32[]{:S(2)}) collective-permute-start(s32[2,4,3]{2,1,0:T(4,128)S(1)} %get-tuple-element.351), channel_id=1, source_target_pairs={{16,0},{32,16},{48,32},{64,48},{80,64},{96,80},{112,96},{0,112},{1... | collective-permute-start | bytes 296 | tf_op jit(solution)/shard_map/while/body/eval_jaxpr/ppermute | solution.py:10
  356.5 2.8 copy.139
  363.6 2.5 reverse_select_fusion.4
  366.1 23.1 %collective-permute-done.1 = s32[4,7]{1,0:T(4,128)S(1)} collective-permute-done((s32[4,7]{1,0:T(4,128)S(1)}, s32[4,7]{1,0:T(4,128)S(1)}, u32[]{:S(2)}, u32[]{:S(2)}) %collective-permute-start.1) | collective-permute-done | bytes 144 | tf_op jit(solution)/shard_map/while/body/eval_jaxpr/ppermute | solution.py:10
  390.5 2.8 copy.139
  397.5 7.8 %collective-permute-done.3 = s32[2,4,3]{2,1,0:T(4,128)S(1)} collective-permute-done((s32[2,4,3]{2,1,0:T(4,128)S(1)}, s32[2,4,3]{2,1,0:T(4,128)S(1)}, u32[]{:S(2)}, u32[]{:S(2)}) %collective-permute-start.3) | collective-permute-done | bytes 128 | tf_op jit(solution)/shard_map/while/body/eval_jaxpr/ppermute | solution.py:10
  405.3 2.5 reverse_select_fusion.4
  407.9 3.0 collective-permute-start.2
  410.9 19.9 %collective-permute-start.3 = (s32[2,4,3]{2,1,0:T(4,128)S(1)}, s32[2,4,3]{2,1,0:T(4,128)S(1)}, u32[]{:S(2)}, u32[]{:S(2)}) collective-permute-start(s32[2,4,3]{2,1,0:T(4,128)S(1)} %get-tuple-element.351), channel_id=1, source_target_pairs={{16,0},{32,16},{48,32},{64,48},{80,64},{96,80},{112,96},{0,112},{1... | collective-permute-start | bytes 296 | tf_op jit(solution)/shard_map/while/body/eval_jaxpr/ppermute | solution.py:10
  432.1 2.8 copy.139
  439.1 2.5 reverse_select_fusion.4
  441.7 20.4 %collective-permute-done.1 = s32[4,7]{1,0:T(4,128)S(1)} collective-permute-done((s32[4,7]{1,0:T(4,128)S(1)}, s32[4,7]{1,0:T(4,128)S(1)}, u32[]{:S(2)}, u32[]{:S(2)}) %collective-permute-start.1) | collective-permute-done | bytes 144 | tf_op jit(solution)/shard_map/while/body/eval_jaxpr/ppermute | solution.py:10
  463.4 2.8 copy.139
  470.4 7.8 %collective-permute-done.3 = s32[2,4,3]{2,1,0:T(4,128)S(1)} collective-permute-done((s32[2,4,3]{2,1,0:T(4,128)S(1)}, s32[2,4,3]{2,1,0:T(4,128)S(1)}, u32[]{:S(2)}, u32[]{:S(2)}) %collective-permute-start.3) | collective-permute-done | bytes 128 | tf_op jit(solution)/shard_map/while/body/eval_jaxpr/ppermute | solution.py:10
  478.3 2.5 reverse_select_fusion.4
  480.8 3.0 collective-permute-start.2
  483.8 19.9 %collective-permute-start.3 = (s32[2,4,3]{2,1,0:T(4,128)S(1)}, s32[2,4,3]{2,1,0:T(4,128)S(1)}, u32[]{:S(2)}, u32[]{:S(2)}) collective-permute-start(s32[2,4,3]{2,1,0:T(4,128)S(1)} %get-tuple-element.351), channel_id=1, source_target_pairs={{16,0},{32,16},{48,32},{64,48},{80,64},{96,80},{112,96},{0,112},{1... | collective-permute-start | bytes 296 | tf_op jit(solution)/shard_map/while/body/eval_jaxpr/ppermute | solution.py:10
  505.0 2.8 copy.139
  512.0 2.5 reverse_select_fusion.4
  514.6 23.1 %collective-permute-done.1 = s32[4,7]{1,0:T(4,128)S(1)} collective-permute-done((s32[4,7]{1,0:T(4,128)S(1)}, s32[4,7]{1,0:T(4,128)S(1)}, u32[]{:S(2)}, u32[]{:S(2)}) %collective-permute-start.1) | collective-permute-done | bytes 144 | tf_op jit(solution)/shard_map/while/body/eval_jaxpr/ppermute | solution.py:10
  539.0 2.8 copy.139
  546.0 4.4 collective-permute-done.3
  550.4 2.5 reverse_select_fusion.4
  558.3 2.9 fusion.16
  563.0 20.2 %all_to_all.5 = bf16[1,1,16,2,128,128]{5,4,3,1,0,2:T(8,128)(2,1)S(1)} all-to-all(bf16[1,1,16,2,128,128]{5,4,3,1,0,2:T(8,128)(2,1)S(1)} %copy.77), channel_id=1, replica_groups=mesh['row'=8,'col'=16] {'col'}, dimensions={2} | all-to-all | bytes 2097152 | tf_op jit(solution)/shard_map/all_to_all | solution.py:68
  (350 shorter events, 94.9 us)
Async XLA Ops:
  0.0 3.7 copy-start.3
  0.0 3.6 copy-start.4
  0.0 3.2 copy-start.2
  0.0 3.4 copy-start.5
  3.7 32.0 %collective-permute-start.2 = (bf16[2,4,3,128,128]{4,3,2,1,0:T(8,128)(2,1)}, bf16[2,4,3,128,128]{4,3,2,1,0:T(8,128)(2,1)}, u32[]{:S(2)}, u32[]{:S(2)}) collective-permute-start(bf16[2,4,3,128,128]{4,3,2,1,0:T(8,128)(2,1)} %get-tuple-element.350), channel_id=1, source_target_pairs={{16,0},{32,16},{48,32},{64,48},{80,64},{96,80},{112,96},{0,112},{1... | collective-permute-start | bytes 2359304 | tf_op jit(solution)/shard_map/while/body/eval_jaxpr/ppermute | solution.py:10
  10.4 25.3 %collective-permute-start.3 = (s32[2,4,3]{2,1,0:T(4,128)S(1)}, s32[2,4,3]{2,1,0:T(4,128)S(1)}, u32[]{:S(2)}, u32[]{:S(2)}) collective-permute-start(s32[2,4,3]{2,1,0:T(4,128)S(1)} %get-tuple-element.351), channel_id=1, source_target_pairs={{16,0},{32,16},{48,32},{64,48},{80,64},{96,80},{112,96},{0,112},{1... | collective-permute-start | bytes 296 | tf_op jit(solution)/shard_map/while/body/eval_jaxpr/ppermute | solution.py:10
  11.6 35.0 %collective-permute-start = (bf16[4,7,128,128]{3,2,1,0:T(8,128)(2,1)S(1)}, bf16[4,7,128,128]{3,2,1,0:T(8,128)(2,1)}, u32[]{:S(2)}, u32[]{:S(2)}) collective-permute-start(bf16[4,7,128,128]{3,2,1,0:T(8,128)(2,1)S(1)} %copy.147), channel_id=1, source_target_pairs={{1,0},{2,1},{3,2},{4,3},{5,4},{6,5},{7,6},{8,7},{9,8},{10,9},{11,1... | collective-permute-start | bytes 2752520 | tf_op jit(solution)/shard_map/while/body/eval_jaxpr/ppermute | solution.py:10
  12.6 34.0 %collective-permute-start.1 = (s32[4,7]{1,0:T(4,128)S(1)}, s32[4,7]{1,0:T(4,128)S(1)}, u32[]{:S(2)}, u32[]{:S(2)}) collective-permute-start(s32[4,7]{1,0:T(4,128)S(1)} %copy.148), channel_id=1, source_target_pairs={{1,0},{2,1},{3,2},{4,3},{5,4},{6,5},{7,6},{8,7},{9,8},{10,9},{11,1... | collective-permute-start | bytes 344 | tf_op jit(solution)/shard_map/while/body/eval_jaxpr/ppermute | solution.py:10
  46.7 26.6 %collective-permute-start.2 = (bf16[2,4,3,128,128]{4,3,2,1,0:T(8,128)(2,1)}, bf16[2,4,3,128,128]{4,3,2,1,0:T(8,128)(2,1)}, u32[]{:S(2)}, u32[]{:S(2)}) collective-permute-start(bf16[2,4,3,128,128]{4,3,2,1,0:T(8,128)(2,1)} %get-tuple-element.350), channel_id=1, source_target_pairs={{16,0},{32,16},{48,32},{64,48},{80,64},{96,80},{112,96},{0,112},{1... | collective-permute-start | bytes 2359304 | tf_op jit(solution)/shard_map/while/body/eval_jaxpr/ppermute | solution.py:10
  46.7 26.5 %collective-permute-start.3 = (s32[2,4,3]{2,1,0:T(4,128)S(1)}, s32[2,4,3]{2,1,0:T(4,128)S(1)}, u32[]{:S(2)}, u32[]{:S(2)}) collective-permute-start(s32[2,4,3]{2,1,0:T(4,128)S(1)} %get-tuple-element.351), channel_id=1, source_target_pairs={{16,0},{32,16},{48,32},{64,48},{80,64},{96,80},{112,96},{0,112},{1... | collective-permute-start | bytes 296 | tf_op jit(solution)/shard_map/while/body/eval_jaxpr/ppermute | solution.py:10
  54.2 38.3 %collective-permute-start = (bf16[4,7,128,128]{3,2,1,0:T(8,128)(2,1)S(1)}, bf16[4,7,128,128]{3,2,1,0:T(8,128)(2,1)}, u32[]{:S(2)}, u32[]{:S(2)}) collective-permute-start(bf16[4,7,128,128]{3,2,1,0:T(8,128)(2,1)S(1)} %copy.147), channel_id=1, source_target_pairs={{1,0},{2,1},{3,2},{4,3},{5,4},{6,5},{7,6},{8,7},{9,8},{10,9},{11,1... | collective-permute-start | bytes 2752520 | tf_op jit(solution)/shard_map/while/body/eval_jaxpr/ppermute | solution.py:10
  54.2 38.3 %collective-permute-start.1 = (s32[4,7]{1,0:T(4,128)S(1)}, s32[4,7]{1,0:T(4,128)S(1)}, u32[]{:S(2)}, u32[]{:S(2)}) collective-permute-start(s32[4,7]{1,0:T(4,128)S(1)} %copy.148), channel_id=1, source_target_pairs={{1,0},{2,1},{3,2},{4,3},{5,4},{6,5},{7,6},{8,7},{9,8},{10,9},{11,1... | collective-permute-start | bytes 344 | tf_op jit(solution)/shard_map/while/body/eval_jaxpr/ppermute | solution.py:10
  92.5 16.3 %collective-permute-start.2 = (bf16[2,4,3,128,128]{4,3,2,1,0:T(8,128)(2,1)}, bf16[2,4,3,128,128]{4,3,2,1,0:T(8,128)(2,1)}, u32[]{:S(2)}, u32[]{:S(2)}) collective-permute-start(bf16[2,4,3,128,128]{4,3,2,1,0:T(8,128)(2,1)} %get-tuple-element.350), channel_id=1, source_target_pairs={{16,0},{32,16},{48,32},{64,48},{80,64},{96,80},{112,96},{0,112},{1... | collective-permute-start | bytes 2359304 | tf_op jit(solution)/shard_map/while/body/eval_jaxpr/ppermute | solution.py:10
  92.5 16.3 %collective-permute-start.3 = (s32[2,4,3]{2,1,0:T(4,128)S(1)}, s32[2,4,3]{2,1,0:T(4,128)S(1)}, u32[]{:S(2)}, u32[]{:S(2)}) collective-permute-start(s32[2,4,3]{2,1,0:T(4,128)S(1)} %get-tuple-element.351), channel_id=1, source_target_pairs={{16,0},{32,16},{48,32},{64,48},{80,64},{96,80},{112,96},{0,112},{1... | collective-permute-start | bytes 296 | tf_op jit(solution)/shard_map/while/body/eval_jaxpr/ppermute | solution.py:10
  93.7 17.7 %collective-permute-start = (bf16[4,7,128,128]{3,2,1,0:T(8,128)(2,1)S(1)}, bf16[4,7,128,128]{3,2,1,0:T(8,128)(2,1)}, u32[]{:S(2)}, u32[]{:S(2)}) collective-permute-start(bf16[4,7,128,128]{3,2,1,0:T(8,128)(2,1)S(1)} %copy.147), channel_id=1, source_target_pairs={{1,0},{2,1},{3,2},{4,3},{5,4},{6,5},{7,6},{8,7},{9,8},{10,9},{11,1... | collective-permute-start | bytes 2752520 | tf_op jit(solution)/shard_map/while/body/eval_jaxpr/ppermute | solution.py:10
  93.7 17.7 %collective-permute-start.1 = (s32[4,7]{1,0:T(4,128)S(1)}, s32[4,7]{1,0:T(4,128)S(1)}, u32[]{:S(2)}, u32[]{:S(2)}) collective-permute-start(s32[4,7]{1,0:T(4,128)S(1)} %copy.148), channel_id=1, source_target_pairs={{1,0},{2,1},{3,2},{4,3},{5,4},{6,5},{7,6},{8,7},{9,8},{10,9},{11,1... | collective-permute-start | bytes 344 | tf_op jit(solution)/shard_map/while/body/eval_jaxpr/ppermute | solution.py:10
  111.4 31.1 %collective-permute-start.2 = (bf16[2,4,3,128,128]{4,3,2,1,0:T(8,128)(2,1)}, bf16[2,4,3,128,128]{4,3,2,1,0:T(8,128)(2,1)}, u32[]{:S(2)}, u32[]{:S(2)}) collective-permute-start(bf16[2,4,3,128,128]{4,3,2,1,0:T(8,128)(2,1)} %get-tuple-element.350), channel_id=1, source_target_pairs={{16,0},{32,16},{48,32},{64,48},{80,64},{96,80},{112,96},{0,112},{1... | collective-permute-start | bytes 2359304 | tf_op jit(solution)/shard_map/while/body/eval_jaxpr/ppermute | solution.py:10
  114.7 27.7 %collective-permute-start.3 = (s32[2,4,3]{2,1,0:T(4,128)S(1)}, s32[2,4,3]{2,1,0:T(4,128)S(1)}, u32[]{:S(2)}, u32[]{:S(2)}) collective-permute-start(s32[2,4,3]{2,1,0:T(4,128)S(1)} %get-tuple-element.351), channel_id=1, source_target_pairs={{16,0},{32,16},{48,32},{64,48},{80,64},{96,80},{112,96},{0,112},{1... | collective-permute-start | bytes 296 | tf_op jit(solution)/shard_map/while/body/eval_jaxpr/ppermute | solution.py:10
  135.3 29.8 %collective-permute-start = (bf16[4,7,128,128]{3,2,1,0:T(8,128)(2,1)S(1)}, bf16[4,7,128,128]{3,2,1,0:T(8,128)(2,1)}, u32[]{:S(2)}, u32[]{:S(2)}) collective-permute-start(bf16[4,7,128,128]{3,2,1,0:T(8,128)(2,1)S(1)} %copy.147), channel_id=1, source_target_pairs={{1,0},{2,1},{3,2},{4,3},{5,4},{6,5},{7,6},{8,7},{9,8},{10,9},{11,1... | collective-permute-start | bytes 2752520 | tf_op jit(solution)/shard_map/while/body/eval_jaxpr/ppermute | solution.py:10
  135.3 29.8 %collective-permute-start.1 = (s32[4,7]{1,0:T(4,128)S(1)}, s32[4,7]{1,0:T(4,128)S(1)}, u32[]{:S(2)}, u32[]{:S(2)}) collective-permute-start(s32[4,7]{1,0:T(4,128)S(1)} %copy.148), channel_id=1, source_target_pairs={{1,0},{2,1},{3,2},{4,3},{5,4},{6,5},{7,6},{8,7},{9,8},{10,9},{11,1... | collective-permute-start | bytes 344 | tf_op jit(solution)/shard_map/while/body/eval_jaxpr/ppermute | solution.py:10
  165.1 16.2 %collective-permute-start.2 = (bf16[2,4,3,128,128]{4,3,2,1,0:T(8,128)(2,1)}, bf16[2,4,3,128,128]{4,3,2,1,0:T(8,128)(2,1)}, u32[]{:S(2)}, u32[]{:S(2)}) collective-permute-start(bf16[2,4,3,128,128]{4,3,2,1,0:T(8,128)(2,1)} %get-tuple-element.350), channel_id=1, source_target_pairs={{16,0},{32,16},{48,32},{64,48},{80,64},{96,80},{112,96},{0,112},{1... | collective-permute-start | bytes 2359304 | tf_op jit(solution)/shard_map/while/body/eval_jaxpr/ppermute | solution.py:10
  165.1 16.1 %collective-permute-start.3 = (s32[2,4,3]{2,1,0:T(4,128)S(1)}, s32[2,4,3]{2,1,0:T(4,128)S(1)}, u32[]{:S(2)}, u32[]{:S(2)}) collective-permute-start(s32[2,4,3]{2,1,0:T(4,128)S(1)} %get-tuple-element.351), channel_id=1, source_target_pairs={{16,0},{32,16},{48,32},{64,48},{80,64},{96,80},{112,96},{0,112},{1... | collective-permute-start | bytes 296 | tf_op jit(solution)/shard_map/while/body/eval_jaxpr/ppermute | solution.py:10
  166.3 17.5 %collective-permute-start = (bf16[4,7,128,128]{3,2,1,0:T(8,128)(2,1)S(1)}, bf16[4,7,128,128]{3,2,1,0:T(8,128)(2,1)}, u32[]{:S(2)}, u32[]{:S(2)}) collective-permute-start(bf16[4,7,128,128]{3,2,1,0:T(8,128)(2,1)S(1)} %copy.147), channel_id=1, source_target_pairs={{1,0},{2,1},{3,2},{4,3},{5,4},{6,5},{7,6},{8,7},{9,8},{10,9},{11,1... | collective-permute-start | bytes 2752520 | tf_op jit(solution)/shard_map/while/body/eval_jaxpr/ppermute | solution.py:10
  166.3 17.5 %collective-permute-start.1 = (s32[4,7]{1,0:T(4,128)S(1)}, s32[4,7]{1,0:T(4,128)S(1)}, u32[]{:S(2)}, u32[]{:S(2)}) collective-permute-start(s32[4,7]{1,0:T(4,128)S(1)} %copy.148), channel_id=1, source_target_pairs={{1,0},{2,1},{3,2},{4,3},{5,4},{6,5},{7,6},{8,7},{9,8},{10,9},{11,1... | collective-permute-start | bytes 344 | tf_op jit(solution)/shard_map/while/body/eval_jaxpr/ppermute | solution.py:10
  183.8 31.2 %collective-permute-start.2 = (bf16[2,4,3,128,128]{4,3,2,1,0:T(8,128)(2,1)}, bf16[2,4,3,128,128]{4,3,2,1,0:T(8,128)(2,1)}, u32[]{:S(2)}, u32[]{:S(2)}) collective-permute-start(bf16[2,4,3,128,128]{4,3,2,1,0:T(8,128)(2,1)} %get-tuple-element.350), channel_id=1, source_target_pairs={{16,0},{32,16},{48,32},{64,48},{80,64},{96,80},{112,96},{0,112},{1... | collective-permute-start | bytes 2359304 | tf_op jit(solution)/shard_map/while/body/eval_jaxpr/ppermute | solution.py:10
  183.8 31.2 %collective-permute-start.3 = (s32[2,4,3]{2,1,0:T(4,128)S(1)}, s32[2,4,3]{2,1,0:T(4,128)S(1)}, u32[]{:S(2)}, u32[]{:S(2)}) collective-permute-start(s32[2,4,3]{2,1,0:T(4,128)S(1)} %get-tuple-element.351), channel_id=1, source_target_pairs={{16,0},{32,16},{48,32},{64,48},{80,64},{96,80},{112,96},{0,112},{1... | collective-permute-start | bytes 296 | tf_op jit(solution)/shard_map/while/body/eval_jaxpr/ppermute | solution.py:10
  207.9 32.8 %collective-permute-start = (bf16[4,7,128,128]{3,2,1,0:T(8,128)(2,1)S(1)}, bf16[4,7,128,128]{3,2,1,0:T(8,128)(2,1)}, u32[]{:S(2)}, u32[]{:S(2)}) collective-permute-start(bf16[4,7,128,128]{3,2,1,0:T(8,128)(2,1)S(1)} %copy.147), channel_id=1, source_target_pairs={{1,0},{2,1},{3,2},{4,3},{5,4},{6,5},{7,6},{8,7},{9,8},{10,9},{11,1... | collective-permute-start | bytes 2752520 | tf_op jit(solution)/shard_map/while/body/eval_jaxpr/ppermute | solution.py:10
  207.9 32.8 %collective-permute-start.1 = (s32[4,7]{1,0:T(4,128)S(1)}, s32[4,7]{1,0:T(4,128)S(1)}, u32[]{:S(2)}, u32[]{:S(2)}) collective-permute-start(s32[4,7]{1,0:T(4,128)S(1)} %copy.148), channel_id=1, source_target_pairs={{1,0},{2,1},{3,2},{4,3},{5,4},{6,5},{7,6},{8,7},{9,8},{10,9},{11,1... | collective-permute-start | bytes 344 | tf_op jit(solution)/shard_map/while/body/eval_jaxpr/ppermute | solution.py:10
  240.7 16.2 %collective-permute-start.2 = (bf16[2,4,3,128,128]{4,3,2,1,0:T(8,128)(2,1)}, bf16[2,4,3,128,128]{4,3,2,1,0:T(8,128)(2,1)}, u32[]{:S(2)}, u32[]{:S(2)}) collective-permute-start(bf16[2,4,3,128,128]{4,3,2,1,0:T(8,128)(2,1)} %get-tuple-element.350), channel_id=1, source_target_pairs={{16,0},{32,16},{48,32},{64,48},{80,64},{96,80},{112,96},{0,112},{1... | collective-permute-start | bytes 2359304 | tf_op jit(solution)/shard_map/while/body/eval_jaxpr/ppermute | solution.py:10
  240.7 16.1 %collective-permute-start.3 = (s32[2,4,3]{2,1,0:T(4,128)S(1)}, s32[2,4,3]{2,1,0:T(4,128)S(1)}, u32[]{:S(2)}, u32[]{:S(2)}) collective-permute-start(s32[2,4,3]{2,1,0:T(4,128)S(1)} %get-tuple-element.351), channel_id=1, source_target_pairs={{16,0},{32,16},{48,32},{64,48},{80,64},{96,80},{112,96},{0,112},{1... | collective-permute-start | bytes 296 | tf_op jit(solution)/shard_map/while/body/eval_jaxpr/ppermute | solution.py:10
  241.9 17.5 %collective-permute-start = (bf16[4,7,128,128]{3,2,1,0:T(8,128)(2,1)S(1)}, bf16[4,7,128,128]{3,2,1,0:T(8,128)(2,1)}, u32[]{:S(2)}, u32[]{:S(2)}) collective-permute-start(bf16[4,7,128,128]{3,2,1,0:T(8,128)(2,1)S(1)} %copy.147), channel_id=1, source_target_pairs={{1,0},{2,1},{3,2},{4,3},{5,4},{6,5},{7,6},{8,7},{9,8},{10,9},{11,1... | collective-permute-start | bytes 2752520 | tf_op jit(solution)/shard_map/while/body/eval_jaxpr/ppermute | solution.py:10
  241.9 17.5 %collective-permute-start.1 = (s32[4,7]{1,0:T(4,128)S(1)}, s32[4,7]{1,0:T(4,128)S(1)}, u32[]{:S(2)}, u32[]{:S(2)}) collective-permute-start(s32[4,7]{1,0:T(4,128)S(1)} %copy.148), channel_id=1, source_target_pairs={{1,0},{2,1},{3,2},{4,3},{5,4},{6,5},{7,6},{8,7},{9,8},{10,9},{11,1... | collective-permute-start | bytes 344 | tf_op jit(solution)/shard_map/while/body/eval_jaxpr/ppermute | solution.py:10
  259.4 31.2 %collective-permute-start.2 = (bf16[2,4,3,128,128]{4,3,2,1,0:T(8,128)(2,1)}, bf16[2,4,3,128,128]{4,3,2,1,0:T(8,128)(2,1)}, u32[]{:S(2)}, u32[]{:S(2)}) collective-permute-start(bf16[2,4,3,128,128]{4,3,2,1,0:T(8,128)(2,1)} %get-tuple-element.350), channel_id=1, source_target_pairs={{16,0},{32,16},{48,32},{64,48},{80,64},{96,80},{112,96},{0,112},{1... | collective-permute-start | bytes 2359304 | tf_op jit(solution)/shard_map/while/body/eval_jaxpr/ppermute | solution.py:10
  262.4 28.2 %collective-permute-start.3 = (s32[2,4,3]{2,1,0:T(4,128)S(1)}, s32[2,4,3]{2,1,0:T(4,128)S(1)}, u32[]{:S(2)}, u32[]{:S(2)}) collective-permute-start(s32[2,4,3]{2,1,0:T(4,128)S(1)} %get-tuple-element.351), channel_id=1, source_target_pairs={{16,0},{32,16},{48,32},{64,48},{80,64},{96,80},{112,96},{0,112},{1... | collective-permute-start | bytes 296 | tf_op jit(solution)/shard_map/while/body/eval_jaxpr/ppermute | solution.py:10
  283.5 30.1 %collective-permute-start = (bf16[4,7,128,128]{3,2,1,0:T(8,128)(2,1)S(1)}, bf16[4,7,128,128]{3,2,1,0:T(8,128)(2,1)}, u32[]{:S(2)}, u32[]{:S(2)}) collective-permute-start(bf16[4,7,128,128]{3,2,1,0:T(8,128)(2,1)S(1)} %copy.147), channel_id=1, source_target_pairs={{1,0},{2,1},{3,2},{4,3},{5,4},{6,5},{7,6},{8,7},{9,8},{10,9},{11,1... | collective-permute-start | bytes 2752520 | tf_op jit(solution)/shard_map/while/body/eval_jaxpr/ppermute | solution.py:10
  283.5 30.1 %collective-permute-start.1 = (s32[4,7]{1,0:T(4,128)S(1)}, s32[4,7]{1,0:T(4,128)S(1)}, u32[]{:S(2)}, u32[]{:S(2)}) collective-permute-start(s32[4,7]{1,0:T(4,128)S(1)} %copy.148), channel_id=1, source_target_pairs={{1,0},{2,1},{3,2},{4,3},{5,4},{6,5},{7,6},{8,7},{9,8},{10,9},{11,1... | collective-permute-start | bytes 344 | tf_op jit(solution)/shard_map/while/body/eval_jaxpr/ppermute | solution.py:10
  313.6 16.2 %collective-permute-start.2 = (bf16[2,4,3,128,128]{4,3,2,1,0:T(8,128)(2,1)}, bf16[2,4,3,128,128]{4,3,2,1,0:T(8,128)(2,1)}, u32[]{:S(2)}, u32[]{:S(2)}) collective-permute-start(bf16[2,4,3,128,128]{4,3,2,1,0:T(8,128)(2,1)} %get-tuple-element.350), channel_id=1, source_target_pairs={{16,0},{32,16},{48,32},{64,48},{80,64},{96,80},{112,96},{0,112},{1... | collective-permute-start | bytes 2359304 | tf_op jit(solution)/shard_map/while/body/eval_jaxpr/ppermute | solution.py:10
  313.6 16.1 %collective-permute-start.3 = (s32[2,4,3]{2,1,0:T(4,128)S(1)}, s32[2,4,3]{2,1,0:T(4,128)S(1)}, u32[]{:S(2)}, u32[]{:S(2)}) collective-permute-start(s32[2,4,3]{2,1,0:T(4,128)S(1)} %get-tuple-element.351), channel_id=1, source_target_pairs={{16,0},{32,16},{48,32},{64,48},{80,64},{96,80},{112,96},{0,112},{1... | collective-permute-start | bytes 296 | tf_op jit(solution)/shard_map/while/body/eval_jaxpr/ppermute | solution.py:10
  314.8 17.5 %collective-permute-start = (bf16[4,7,128,128]{3,2,1,0:T(8,128)(2,1)S(1)}, bf16[4,7,128,128]{3,2,1,0:T(8,128)(2,1)}, u32[]{:S(2)}, u32[]{:S(2)}) collective-permute-start(bf16[4,7,128,128]{3,2,1,0:T(8,128)(2,1)S(1)} %copy.147), channel_id=1, source_target_pairs={{1,0},{2,1},{3,2},{4,3},{5,4},{6,5},{7,6},{8,7},{9,8},{10,9},{11,1... | collective-permute-start | bytes 2752520 | tf_op jit(solution)/shard_map/while/body/eval_jaxpr/ppermute | solution.py:10
  314.8 17.5 %collective-permute-start.1 = (s32[4,7]{1,0:T(4,128)S(1)}, s32[4,7]{1,0:T(4,128)S(1)}, u32[]{:S(2)}, u32[]{:S(2)}) collective-permute-start(s32[4,7]{1,0:T(4,128)S(1)} %copy.148), channel_id=1, source_target_pairs={{1,0},{2,1},{3,2},{4,3},{5,4},{6,5},{7,6},{8,7},{9,8},{10,9},{11,1... | collective-permute-start | bytes 344 | tf_op jit(solution)/shard_map/while/body/eval_jaxpr/ppermute | solution.py:10
  332.3 31.2 %collective-permute-start.2 = (bf16[2,4,3,128,128]{4,3,2,1,0:T(8,128)(2,1)}, bf16[2,4,3,128,128]{4,3,2,1,0:T(8,128)(2,1)}, u32[]{:S(2)}, u32[]{:S(2)}) collective-permute-start(bf16[2,4,3,128,128]{4,3,2,1,0:T(8,128)(2,1)} %get-tuple-element.350), channel_id=1, source_target_pairs={{16,0},{32,16},{48,32},{64,48},{80,64},{96,80},{112,96},{0,112},{1... | collective-permute-start | bytes 2359304 | tf_op jit(solution)/shard_map/while/body/eval_jaxpr/ppermute | solution.py:10
  335.3 28.2 %collective-permute-start.3 = (s32[2,4,3]{2,1,0:T(4,128)S(1)}, s32[2,4,3]{2,1,0:T(4,128)S(1)}, u32[]{:S(2)}, u32[]{:S(2)}) collective-permute-start(s32[2,4,3]{2,1,0:T(4,128)S(1)} %get-tuple-element.351), channel_id=1, source_target_pairs={{16,0},{32,16},{48,32},{64,48},{80,64},{96,80},{112,96},{0,112},{1... | collective-permute-start | bytes 296 | tf_op jit(solution)/shard_map/while/body/eval_jaxpr/ppermute | solution.py:10
  356.4 32.8 %collective-permute-start = (bf16[4,7,128,128]{3,2,1,0:T(8,128)(2,1)S(1)}, bf16[4,7,128,128]{3,2,1,0:T(8,128)(2,1)}, u32[]{:S(2)}, u32[]{:S(2)}) collective-permute-start(bf16[4,7,128,128]{3,2,1,0:T(8,128)(2,1)S(1)} %copy.147), channel_id=1, source_target_pairs={{1,0},{2,1},{3,2},{4,3},{5,4},{6,5},{7,6},{8,7},{9,8},{10,9},{11,1... | collective-permute-start | bytes 2752520 | tf_op jit(solution)/shard_map/while/body/eval_jaxpr/ppermute | solution.py:10
  356.4 32.8 %collective-permute-start.1 = (s32[4,7]{1,0:T(4,128)S(1)}, s32[4,7]{1,0:T(4,128)S(1)}, u32[]{:S(2)}, u32[]{:S(2)}) collective-permute-start(s32[4,7]{1,0:T(4,128)S(1)} %copy.148), channel_id=1, source_target_pairs={{1,0},{2,1},{3,2},{4,3},{5,4},{6,5},{7,6},{8,7},{9,8},{10,9},{11,1... | collective-permute-start | bytes 344 | tf_op jit(solution)/shard_map/while/body/eval_jaxpr/ppermute | solution.py:10
  389.2 16.2 %collective-permute-start.2 = (bf16[2,4,3,128,128]{4,3,2,1,0:T(8,128)(2,1)}, bf16[2,4,3,128,128]{4,3,2,1,0:T(8,128)(2,1)}, u32[]{:S(2)}, u32[]{:S(2)}) collective-permute-start(bf16[2,4,3,128,128]{4,3,2,1,0:T(8,128)(2,1)} %get-tuple-element.350), channel_id=1, source_target_pairs={{16,0},{32,16},{48,32},{64,48},{80,64},{96,80},{112,96},{0,112},{1... | collective-permute-start | bytes 2359304 | tf_op jit(solution)/shard_map/while/body/eval_jaxpr/ppermute | solution.py:10
  389.2 16.1 %collective-permute-start.3 = (s32[2,4,3]{2,1,0:T(4,128)S(1)}, s32[2,4,3]{2,1,0:T(4,128)S(1)}, u32[]{:S(2)}, u32[]{:S(2)}) collective-permute-start(s32[2,4,3]{2,1,0:T(4,128)S(1)} %get-tuple-element.351), channel_id=1, source_target_pairs={{16,0},{32,16},{48,32},{64,48},{80,64},{96,80},{112,96},{0,112},{1... | collective-permute-start | bytes 296 | tf_op jit(solution)/shard_map/while/body/eval_jaxpr/ppermute | solution.py:10
  390.4 17.5 %collective-permute-start = (bf16[4,7,128,128]{3,2,1,0:T(8,128)(2,1)S(1)}, bf16[4,7,128,128]{3,2,1,0:T(8,128)(2,1)}, u32[]{:S(2)}, u32[]{:S(2)}) collective-permute-start(bf16[4,7,128,128]{3,2,1,0:T(8,128)(2,1)S(1)} %copy.147), channel_id=1, source_target_pairs={{1,0},{2,1},{3,2},{4,3},{5,4},{6,5},{7,6},{8,7},{9,8},{10,9},{11,1... | collective-permute-start | bytes 2752520 | tf_op jit(solution)/shard_map/while/body/eval_jaxpr/ppermute | solution.py:10
  390.4 17.5 %collective-permute-start.1 = (s32[4,7]{1,0:T(4,128)S(1)}, s32[4,7]{1,0:T(4,128)S(1)}, u32[]{:S(2)}, u32[]{:S(2)}) collective-permute-start(s32[4,7]{1,0:T(4,128)S(1)} %copy.148), channel_id=1, source_target_pairs={{1,0},{2,1},{3,2},{4,3},{5,4},{6,5},{7,6},{8,7},{9,8},{10,9},{11,1... | collective-permute-start | bytes 344 | tf_op jit(solution)/shard_map/while/body/eval_jaxpr/ppermute | solution.py:10
  407.9 31.2 %collective-permute-start.2 = (bf16[2,4,3,128,128]{4,3,2,1,0:T(8,128)(2,1)}, bf16[2,4,3,128,128]{4,3,2,1,0:T(8,128)(2,1)}, u32[]{:S(2)}, u32[]{:S(2)}) collective-permute-start(bf16[2,4,3,128,128]{4,3,2,1,0:T(8,128)(2,1)} %get-tuple-element.350), channel_id=1, source_target_pairs={{16,0},{32,16},{48,32},{64,48},{80,64},{96,80},{112,96},{0,112},{1... | collective-permute-start | bytes 2359304 | tf_op jit(solution)/shard_map/while/body/eval_jaxpr/ppermute | solution.py:10
  410.9 28.2 %collective-permute-start.3 = (s32[2,4,3]{2,1,0:T(4,128)S(1)}, s32[2,4,3]{2,1,0:T(4,128)S(1)}, u32[]{:S(2)}, u32[]{:S(2)}) collective-permute-start(s32[2,4,3]{2,1,0:T(4,128)S(1)} %get-tuple-element.351), channel_id=1, source_target_pairs={{16,0},{32,16},{48,32},{64,48},{80,64},{96,80},{112,96},{0,112},{1... | collective-permute-start | bytes 296 | tf_op jit(solution)/shard_map/while/body/eval_jaxpr/ppermute | solution.py:10
  432.0 30.1 %collective-permute-start = (bf16[4,7,128,128]{3,2,1,0:T(8,128)(2,1)S(1)}, bf16[4,7,128,128]{3,2,1,0:T(8,128)(2,1)}, u32[]{:S(2)}, u32[]{:S(2)}) collective-permute-start(bf16[4,7,128,128]{3,2,1,0:T(8,128)(2,1)S(1)} %copy.147), channel_id=1, source_target_pairs={{1,0},{2,1},{3,2},{4,3},{5,4},{6,5},{7,6},{8,7},{9,8},{10,9},{11,1... | collective-permute-start | bytes 2752520 | tf_op jit(solution)/shard_map/while/body/eval_jaxpr/ppermute | solution.py:10
  432.0 30.1 %collective-permute-start.1 = (s32[4,7]{1,0:T(4,128)S(1)}, s32[4,7]{1,0:T(4,128)S(1)}, u32[]{:S(2)}, u32[]{:S(2)}) collective-permute-start(s32[4,7]{1,0:T(4,128)S(1)} %copy.148), channel_id=1, source_target_pairs={{1,0},{2,1},{3,2},{4,3},{5,4},{6,5},{7,6},{8,7},{9,8},{10,9},{11,1... | collective-permute-start | bytes 344 | tf_op jit(solution)/shard_map/while/body/eval_jaxpr/ppermute | solution.py:10
  462.1 16.2 %collective-permute-start.2 = (bf16[2,4,3,128,128]{4,3,2,1,0:T(8,128)(2,1)}, bf16[2,4,3,128,128]{4,3,2,1,0:T(8,128)(2,1)}, u32[]{:S(2)}, u32[]{:S(2)}) collective-permute-start(bf16[2,4,3,128,128]{4,3,2,1,0:T(8,128)(2,1)} %get-tuple-element.350), channel_id=1, source_target_pairs={{16,0},{32,16},{48,32},{64,48},{80,64},{96,80},{112,96},{0,112},{1... | collective-permute-start | bytes 2359304 | tf_op jit(solution)/shard_map/while/body/eval_jaxpr/ppermute | solution.py:10
  462.1 16.1 %collective-permute-start.3 = (s32[2,4,3]{2,1,0:T(4,128)S(1)}, s32[2,4,3]{2,1,0:T(4,128)S(1)}, u32[]{:S(2)}, u32[]{:S(2)}) collective-permute-start(s32[2,4,3]{2,1,0:T(4,128)S(1)} %get-tuple-element.351), channel_id=1, source_target_pairs={{16,0},{32,16},{48,32},{64,48},{80,64},{96,80},{112,96},{0,112},{1... | collective-permute-start | bytes 296 | tf_op jit(solution)/shard_map/while/body/eval_jaxpr/ppermute | solution.py:10
  463.3 17.5 %collective-permute-start = (bf16[4,7,128,128]{3,2,1,0:T(8,128)(2,1)S(1)}, bf16[4,7,128,128]{3,2,1,0:T(8,128)(2,1)}, u32[]{:S(2)}, u32[]{:S(2)}) collective-permute-start(bf16[4,7,128,128]{3,2,1,0:T(8,128)(2,1)S(1)} %copy.147), channel_id=1, source_target_pairs={{1,0},{2,1},{3,2},{4,3},{5,4},{6,5},{7,6},{8,7},{9,8},{10,9},{11,1... | collective-permute-start | bytes 2752520 | tf_op jit(solution)/shard_map/while/body/eval_jaxpr/ppermute | solution.py:10
  463.3 17.5 %collective-permute-start.1 = (s32[4,7]{1,0:T(4,128)S(1)}, s32[4,7]{1,0:T(4,128)S(1)}, u32[]{:S(2)}, u32[]{:S(2)}) collective-permute-start(s32[4,7]{1,0:T(4,128)S(1)} %copy.148), channel_id=1, source_target_pairs={{1,0},{2,1},{3,2},{4,3},{5,4},{6,5},{7,6},{8,7},{9,8},{10,9},{11,1... | collective-permute-start | bytes 344 | tf_op jit(solution)/shard_map/while/body/eval_jaxpr/ppermute | solution.py:10
  480.8 31.2 %collective-permute-start.2 = (bf16[2,4,3,128,128]{4,3,2,1,0:T(8,128)(2,1)}, bf16[2,4,3,128,128]{4,3,2,1,0:T(8,128)(2,1)}, u32[]{:S(2)}, u32[]{:S(2)}) collective-permute-start(bf16[2,4,3,128,128]{4,3,2,1,0:T(8,128)(2,1)} %get-tuple-element.350), channel_id=1, source_target_pairs={{16,0},{32,16},{48,32},{64,48},{80,64},{96,80},{112,96},{0,112},{1... | collective-permute-start | bytes 2359304 | tf_op jit(solution)/shard_map/while/body/eval_jaxpr/ppermute | solution.py:10
  483.8 28.2 %collective-permute-start.3 = (s32[2,4,3]{2,1,0:T(4,128)S(1)}, s32[2,4,3]{2,1,0:T(4,128)S(1)}, u32[]{:S(2)}, u32[]{:S(2)}) collective-permute-start(s32[2,4,3]{2,1,0:T(4,128)S(1)} %get-tuple-element.351), channel_id=1, source_target_pairs={{16,0},{32,16},{48,32},{64,48},{80,64},{96,80},{112,96},{0,112},{1... | collective-permute-start | bytes 296 | tf_op jit(solution)/shard_map/while/body/eval_jaxpr/ppermute | solution.py:10
  504.9 32.8 %collective-permute-start = (bf16[4,7,128,128]{3,2,1,0:T(8,128)(2,1)S(1)}, bf16[4,7,128,128]{3,2,1,0:T(8,128)(2,1)}, u32[]{:S(2)}, u32[]{:S(2)}) collective-permute-start(bf16[4,7,128,128]{3,2,1,0:T(8,128)(2,1)S(1)} %copy.147), channel_id=1, source_target_pairs={{1,0},{2,1},{3,2},{4,3},{5,4},{6,5},{7,6},{8,7},{9,8},{10,9},{11,1... | collective-permute-start | bytes 2752520 | tf_op jit(solution)/shard_map/while/body/eval_jaxpr/ppermute | solution.py:10
  504.9 32.8 %collective-permute-start.1 = (s32[4,7]{1,0:T(4,128)S(1)}, s32[4,7]{1,0:T(4,128)S(1)}, u32[]{:S(2)}, u32[]{:S(2)}) collective-permute-start(s32[4,7]{1,0:T(4,128)S(1)} %copy.148), channel_id=1, source_target_pairs={{1,0},{2,1},{3,2},{4,3},{5,4},{6,5},{7,6},{8,7},{9,8},{10,9},{11,1... | collective-permute-start | bytes 344 | tf_op jit(solution)/shard_map/while/body/eval_jaxpr/ppermute | solution.py:10
  537.7 12.7 %collective-permute-start.2 = (bf16[2,4,3,128,128]{4,3,2,1,0:T(8,128)(2,1)}, bf16[2,4,3,128,128]{4,3,2,1,0:T(8,128)(2,1)}, u32[]{:S(2)}, u32[]{:S(2)}) collective-permute-start(bf16[2,4,3,128,128]{4,3,2,1,0:T(8,128)(2,1)} %get-tuple-element.350), channel_id=1, source_target_pairs={{16,0},{32,16},{48,32},{64,48},{80,64},{96,80},{112,96},{0,112},{1... | collective-permute-start | bytes 2359304 | tf_op jit(solution)/shard_map/while/body/eval_jaxpr/ppermute | solution.py:10
  537.7 12.7 %collective-permute-start.3 = (s32[2,4,3]{2,1,0:T(4,128)S(1)}, s32[2,4,3]{2,1,0:T(4,128)S(1)}, u32[]{:S(2)}, u32[]{:S(2)}) collective-permute-start(s32[2,4,3]{2,1,0:T(4,128)S(1)} %get-tuple-element.351), channel_id=1, source_target_pairs={{16,0},{32,16},{48,32},{64,48},{80,64},{96,80},{112,96},{0,112},{1... | collective-permute-start | bytes 296 | tf_op jit(solution)/shard_map/while/body/eval_jaxpr/ppermute | solution.py:10
  538.9 14.1 %collective-permute-start = (bf16[4,7,128,128]{3,2,1,0:T(8,128)(2,1)S(1)}, bf16[4,7,128,128]{3,2,1,0:T(8,128)(2,1)}, u32[]{:S(2)}, u32[]{:S(2)}) collective-permute-start(bf16[4,7,128,128]{3,2,1,0:T(8,128)(2,1)S(1)} %copy.147), channel_id=1, source_target_pairs={{1,0},{2,1},{3,2},{4,3},{5,4},{6,5},{7,6},{8,7},{9,8},{10,9},{11,1... | collective-permute-start | bytes 2752520 | tf_op jit(solution)/shard_map/while/body/eval_jaxpr/ppermute | solution.py:10
  538.9 14.0 %collective-permute-start.1 = (s32[4,7]{1,0:T(4,128)S(1)}, s32[4,7]{1,0:T(4,128)S(1)}, u32[]{:S(2)}, u32[]{:S(2)}) collective-permute-start(s32[4,7]{1,0:T(4,128)S(1)} %copy.148), channel_id=1, source_target_pairs={{1,0},{2,1},{3,2},{4,3},{5,4},{6,5},{7,6},{8,7},{9,8},{10,9},{11,1... | collective-permute-start | bytes 344 | tf_op jit(solution)/shard_map/while/body/eval_jaxpr/ppermute | solution.py:10
  (17 other events, 26.6 us)
where the time goes:
time: 590 us; the launch traced here: 584 us
  waiting for transfers between devices  232 us (39%)
  starting transfers between devices  154 us (26%)
  local copies, waits for them, and re-layouts  71 us (12%)
  matrix products  62.6 us (11%)
  other arithmetic  42.9 us (7%)
  blocking collectives  20.2 us (3%)
    ppermute x60, waiting for transfers between devices, passed_along(): return lax.ppermute(block, axis, route)  232 us
    ppermute x60, starting transfers between devices, passed_along(): return lax.ppermute(block, axis, route)  154 us
    while x75, local copies, waits for them, and re-layouts  59.5 us
    select_n x15, other arithmetic, advance(): b_pair = jnp.where(last_row, b_pair[::-1], b_pair)  38.2 us
    dot_general x16, matrix products, tile_product(): jnp.einsum('kcrxy,kcyz->rcxz', a_chosen, b_chosen, preferred_element_type...  29.3 us
    dot_general x16, matrix products, tile_product(): jnp.einsum('kabrc,kaxy->kcrxy', combo, a_data, preferred_element_type=jnp...  25.8 us
    all_to_all x1, blocking collectives, on_device(): lax.all_to_all(outgoing[None, None], 'col', split_axis=2, concat_axis=2,...  20.2 us
  transfers between devices with their start and end apart: 60, of which 17 were waited for; matrix products, arithmetic and copies ran while one was open for 28% of the time, Pallas kernels for 0%

commit v1 on v0

v1 whole, which is shorter than its diff:
```python
import functools

import jax
import jax.numpy as jnp
from jax import lax
from jax.experimental import pallas as pl
from jax.experimental.pallas import tpu as pltpu
from jax.sharding import PartitionSpec as P

MESH = pl.DeviceIdType.MESH
BF16, F32, I32 = jnp.bfloat16, jnp.float32, jnp.int32
W = 128

A_PIECES = ((0, 7), (7, 7), (14, 4), (18, 3), (21, 7))
B_PIECES = ((0, 6), (6, 6), (12, 6), (18, 6))
A_HALF = ((0, 1), (2, 3, 4))
UNIT = 0.624


def a_slot(dy, dz, dk):
    return (dy % 4) * 4 + dz * 2 + dk


def b_slot(dx, dz):
    return (dx % 4) * 2 + dz


def a_forwards(dy, dz, p):
    out = []
    if (dy, dz) == (0, 0):
        out += [("y+", a_slot(3, 0, 0)), ("y-", a_slot(1, 0, 0)), ("zl", a_slot(0, 1, 0))]
    elif (dy, dz) == (0, 1):
        if p >= 1:
            out += [("y+", a_slot(3, 1, 0)), ("y-", a_slot(1, 1, 0))]
    elif dz == 0:
        if dy == 3 and p in (0, 1):
            out.append(("y+", a_slot(2, 0, 0)))
        if dy == 1 and p in (2, 3, 4):
            out.append(("y-", a_slot(2, 0, 0)))
        if p == 0:
            out.append(("zl", a_slot(dy, 1, 0)))
    else:
        if dy == 3 and p in (1, 2):
            out.append(("y+", a_slot(2, 1, 0)))
        if dy == 1 and p in (3, 4):
            out.append(("y-", a_slot(2, 1, 0)))
    out.append(("sib", a_slot(dy, dz, 1)))
    return out


def b_forwards(dx, dz, c):
    if (dx, dz) == (0, 0):
        return [("x+", b_slot(3, 0)), ("x-", b_slot(1, 0)), ("zh", b_slot(0, 1))]
    if dx == 0:
        return [("x+", b_slot(3, 1)), ("x-", b_slot(1, 1))]
    if dx == 3 and c in (0, 1):
        return [("x+", b_slot(2, dz))]
    if dx == 1 and c in (2, 3):
        return [("x-", b_slot(2, dz))]
    return []


def arrivals():
    ends = [lo + n for lo, n in A_PIECES]
    out = []

    def a(dy, dz, p, t):
        out.append((t, "A", a_slot(dy, dz, 0), p))
        out.append((t + 2.0, "A", a_slot(dy, dz, 1), p))

    for p in range(5):
        out.append((1.5 + ends[p] * 0.1, "A", a_slot(0, 0, 1), p))
        a(1, 0, p, UNIT * ends[p])
        a(3, 0, p, UNIT * ends[p])
        a(0, 1, p, 2 * UNIT * ends[p] * 0.92)
        a(2, 0, p, UNIT * (28 + (ends[p] if p < 2 else ends[p] - 14)))
        if p:
            a(1, 1, p, UNIT * (42 + ends[p] - 7))
            a(3, 1, p, UNIT * (42 + ends[p] - 7))
            a(2, 1, p, UNIT * (63 + (ends[p] - 7 if p < 3 else ends[p] - 18)))
    a(1, 1, 0, UNIT * 58)
    a(3, 1, 0, UNIT * 60)
    a(2, 1, 0, UNIT * 70)
    for c in range(4):
        e = 6 * (c + 1)
        half = 6 * (c % 2 + 1)
        for dx in (1, 3):
            out.append((UNIT * e, "B", b_slot(dx, 0), c))
            out.append((UNIT * (36 + e), "B", b_slot(dx, 1), c))
        out.append((2 * UNIT * e, "B", b_slot(0, 1), c))
        out.append((UNIT * (24 + half), "B", b_slot(2, 0), c))
        out.append((UNIT * (60 + half), "B", b_slot(2, 1), c))
    return sorted(out, key=lambda r: r[0])


def make_plan(step):
    phases, copies = [[]], []

    def start(kind, slot, piece, phase):
        if kind == "A":
            dy, dz, dk = slot // 4, slot // 2 % 2, slot % 2
            nexts = [] if dk else a_forwards(dy, dz, piece)
        else:
            nexts = b_forwards(slot // 2, slot % 2, piece)
        for target, there in nexts:
            copies.append((phase, kind, slot, there, piece, target))

    for p in range(5):
        start("A", 0, p, 0)
        if p < 4:
            start("B", 0, p, 0)
    last = 0.0
    for t, kind, slot, piece in arrivals():
        if t - last > step or not phases[-1]:
            if phases[-1]:
                last = t
            phases.append([])
            last = t
        phases[-1].append((kind, slot, piece))
        start(kind, slot, piece, len(phases) - 1)
    when_a = [0] * 32
    when_b = [0] * 32
    for n, phase in enumerate(phases):
        for kind, slot, piece in phase:
            if kind == "A":
                at = slot * 2 + (0 if piece in A_HALF[0] else 1)
                when_a[at] = max(when_a[at], n)
            else:
                at = slot * 4 + piece
                when_b[at] = max(when_b[at], n)
    triggers, bounds = [], [0]
    for n in range(len(phases)):
        triggers += [i for i in range(32) if when_a[i] == n]
        triggers += [32 + i for i in range(32) if when_b[i] == n]
        bounds.append(len(triggers))
    return phases, copies, when_a, when_b, triggers, bounds


PHASES, COPIES, WHEN_A, WHEN_B, TRIGGERS, BOUNDS = make_plan(2.4)


def entry(table, at):
    padded = list(table) + [0] * (-len(table) % 4)
    words = [sum(v << (7 * i) for i, v in enumerate(padded[w:w + 4])) for w in range(0, len(padded), 4)]
    which, word = lax.div(at, 4), I32(words[0])
    for i, v in enumerate(words[1:], 1):
        word = jnp.where(which == i, I32(v), word)
    return lax.rem(lax.shift_right_logical(word, 7 * lax.rem(at, 4)), 128)


def kernel(a_in, b_in, a_rows, b_cols, screen, keep, owners, out, a_all, b_all, total, dense, stage, lists, mask, meta_a,
           meta_b, owned_m, owned_f, a_recv, b_recv, sent, ma_send, ma_recv, mb_send, mb_recv, out_send, out_recv, own_sem):
    row, col = lax.axis_index("row"), lax.axis_index("col")
    rem, div = lax.rem, lax.div
    x, zh = div(row, 2), rem(row, 2)
    y, zl, core = div(col, 4), rem(div(col, 2), 2), rem(col, 2)
    targets = {
        "y+": (row, rem(col + 4, 16)),
        "y-": (row, rem(col + 12, 16)),
        "zl": (row, col + 2 - 4 * zl),
        "sib": (row, col + 1 - 2 * core),
        "x+": (rem(row + 2, 8), col),
        "x-": (rem(row + 6, 8), col),
        "zh": (row + 1 - 2 * zh, col),
    }

    barrier = pltpu.get_barrier_semaphore()

    @pl.loop(1, 16)
    def _(t):
        pl.semaphore_signal(barrier, inc=1, device_id=(row, rem(col + t, 16)), device_id_type=MESH)

    @pl.loop(1, 8)
    def _(t):
        pl.semaphore_signal(barrier, inc=1, device_id=(rem(row + t, 8), col), device_id_type=MESH)

    for i in list(range(36, 64)) + list(range(104, W)):
        lists[i] = I32(0)
    for k in range(4):
        gone = I32(28)
        places = [I32(7)] * 8
        for a in range(7):
            at = a_rows[k, a]
            gone = gone - at
            places = [jnp.where(at == r, a, v) for r, v in enumerate(places)]
        for r in range(8):
            lists[k * 8 + r] = places[r]
        lists[32 + k] = gone
    for h in range(2):
        for k in range(4):
            gone = I32(6)
            places = [I32(3)] * 4
            for b in range(3):
                at = b_cols[b, h, k]
                gone = gone - at
                places = [jnp.where(at == c, b, v) for c, v in enumerate(places)]
            for c in range(4):
                lists[64 + h * 16 + k * 4 + c] = places[c]
            lists[96 + h * 4 + k] = gone

    @pl.loop(0, W)
    def _(i):
        meta_a[col, i] = lists[i]
        meta_b[row, i] = lists[i]

    @pl.loop(0, 28)
    def _(i):
        k, n = div(i, 7), rem(i, 7)
        place = n + jnp.where(n >= lists[32 + k], 1, 0)
        a_all[0, i] = a_in[k, jnp.minimum(lists[k * 8 + place], 6)]

    @pl.loop(0, 24)
    def _(i):
        hk, n = div(i, 3), rem(i, 3)
        place = n + jnp.where(n >= lists[96 + hk], 1, 0)
        b_all[0, i] = b_in[hk, jnp.minimum(lists[64 + hk * 4 + place], 2)]

    def copy_of(number):
        _, kind, slot, there, piece, target = COPIES[number]
        ref, pieces, recv = (a_all, A_PIECES, a_recv) if kind == "A" else (b_all, B_PIECES, b_recv)
        lo, n = pieces[piece]
        return pltpu.make_async_remote_copy(
            src_ref=ref.at[slot, pl.ds(lo, n)], dst_ref=ref.at[there, pl.ds(lo, n)],
            send_sem=sent.at[number], recv_sem=recv.at[there * len(pieces) + piece],
            device_id=targets[target], device_id_type=MESH)

    def arrival_of(kind, slot, piece):
        ref, pieces, recv = (a_all, A_PIECES, a_recv) if kind == "A" else (b_all, B_PIECES, b_recv)
        lo, n = pieces[piece]
        there = ref.at[slot, pl.ds(lo, n)]
        return pltpu.make_async_remote_copy(
            src_ref=there, dst_ref=there, send_sem=sent.at[0], recv_sem=recv.at[slot * len(pieces) + piece],
            device_id=targets["sib"], device_id_type=MESH)

    def meta_a_copy(t):
        return pltpu.make_async_remote_copy(
            src_ref=lists, dst_ref=meta_a.at[col], send_sem=ma_send.at[t], recv_sem=ma_recv.at[col],
            device_id=(row, rem(col + t, 16)), device_id_type=MESH)

    def meta_b_copy(t):
        return pltpu.make_async_remote_copy(
            src_ref=lists, dst_ref=meta_b.at[row], send_sem=mb_send.at[t], recv_sem=mb_recv.at[row],
            device_id=(rem(row + t, 8), col), device_id_type=MESH)

    pl.semaphore_wait(barrier, 22)

    for number, copy in enumerate(COPIES):
        if copy[0] == 0:
            copy_of(number).start()

    @pl.loop(1, 16)
    def _(t):
        meta_a_copy(t).start()

    @pl.loop(1, 8)
    def _(t):
        meta_b_copy(t).start()

    @pl.loop(0, 16)
    def _(s):
        for k in range(4):
            for a in range(8):
                for b in range(4):
                    at = (s * 4 + k) * 32 + a * 4 + b
                    mask[at] = screen[a, b, k, s].astype(F32) if a < 7 and b < 3 else F32(0)

    @pl.loop(0, 16)
    def _(o):
        first, last = I32(32), I32(-1)
        for m in range(32):
            here = owners[m] == o
            first = jnp.where(here, jnp.minimum(first, m), first)
            last = jnp.where(here, m, last)
        some, two = last >= 0, last > first
        first = jnp.where(some, first, 0)
        last = jnp.where(two, last, 0)
        owned_m[2 * o] = rem(first, 4) * 8 + div(first, 4)
        owned_m[2 * o + 1] = rem(last, 4) * 8 + div(last, 4)
        owned_f[2 * o] = jnp.where(some, keep[first], 0).astype(F32)
        owned_f[2 * o + 1] = jnp.where(two, keep[last], 0).astype(F32)

    @pl.loop(0, 32)
    def _(m):
        total[m] = jnp.zeros((W, W), F32)

    @pl.loop(1, 16)
    def _(t):
        source = rem(col + t, 16)
        pltpu.make_async_remote_copy(
            src_ref=meta_a.at[source], dst_ref=meta_a.at[source], send_sem=ma_send.at[t], recv_sem=ma_recv.at[source],
            device_id=(row, source), device_id_type=MESH).wait_recv()

    @pl.loop(1, 8)
    def _(t):
        source = rem(row + t, 8)
        pltpu.make_async_remote_copy(
            src_ref=meta_b.at[source], dst_ref=meta_b.at[source], send_sem=mb_send.at[t], recv_sem=mb_recv.at[source],
            device_id=(source, col), device_id_type=MESH).wait_recv()

    def multiply(qa, half, qb, h, s, g, p):
        for kk in range(2):
            k = half * 2 + kk
            gone = meta_a[g, 32 + k]
            for r in range(8):
                low = a_all[qa, k * 7 + min(r, 6)]
                high = a_all[qa, k * 7 + max(r - 1, 0)]
                dense[r * W:(r + 1) * W, kk * W:(kk + 1) * W] = jnp.where(r < gone, low, high)
        for c in range(4):
            right = []
            for kk in range(2):
                hk = h * 4 + half * 2 + kk
                low = b_all[qb, hk * 3 + min(c, 2)]
                high = b_all[qb, hk * 3 + max(c - 1, 0)]
                right.append(jnp.where(c < meta_b[p, 96 + hk], low, high))
            rows = []
            for r in range(8):
                cells = []
                for kk in range(2):
                    k = half * 2 + kk
                    at = (s * 4 + k) * 32 + meta_a[g, k * 8 + r] * 4 + meta_b[p, 64 + h * 16 + k * 4 + c]
                    cells.append(dense[r * W:(r + 1) * W, kk * W:(kk + 1) * W] * mask[at].astype(BF16))
                rows.append(jnp.concatenate(cells, axis=1))
            left = jnp.concatenate(rows, axis=0)
            part = jnp.dot(left, jnp.concatenate(right, axis=0), preferred_element_type=F32)
            total[c * 8:(c + 1) * 8] += part.reshape(8, W, W)

    @pl.loop(0, len(PHASES))
    def _(n):
        for i, phase in enumerate(PHASES):
            if i == 0:
                continue

            @pl.when(n == i)
            def _(i=i, phase=phase):
                for kind, slot, piece in phase:
                    arrival_of(kind, slot, piece).wait_recv()
                    for number, copy in enumerate(COPIES):
                        if copy[0] == i and (copy[1], copy[2], copy[4]) == (kind, slot, piece):
                            copy_of(number).start()

        @pl.loop(entry(BOUNDS, n), entry(BOUNDS, n + 1))
        def _(u):
            code = entry(TRIGGERS, u)
            by_b = div(code, 32)
            index = rem(code, 32)
            half = rem(index, 2)
            which = div(index, 2)
            g_a = 4 * rem(y + div(which, 4), 4) + 2 * rem(zl + rem(div(which, 2), 2), 2) + rem(core + rem(which, 2), 2)
            s_a = rem(g_a - col + 16, 16)
            p_b = 2 * rem(x + div(which, 4), 4) + rem(zh + rem(div(which, 2), 2), 2)
            s_b = rem(p_b + 8 * rem(which, 2) - row + 16, 16)
            s = jnp.where(by_b == 1, s_b, s_a)
            g = rem(col + s, 16)
            e = rem(row + s, 16)
            p, h = rem(e, 8), div(e, 8)
            qa = 4 * rem(div(g, 4) - y + 4, 4) + 2 * rem(rem(div(g, 2), 2) + zl, 2) + rem(rem(g, 2) + core, 2)
            qb = 2 * rem(div(p, 2) - x + 4, 4) + rem(rem(p, 2) + zh, 2)
            when_a = entry(WHEN_A, qa * 2 + half)
            when_b = entry(WHEN_B, qb * 4 + h * 2 + half)
            ready = jnp.where(by_b == 1, when_a < n, when_b <= n)

            @pl.when(ready)
            def _():
                multiply(qa, half, qb, h, s, g, p)

    def out_copy(t):
        o = rem(col + t, 16)
        return pltpu.make_async_remote_copy(
            src_ref=stage.at[t], dst_ref=out.at[col], send_sem=out_send.at[t], recv_sem=out_recv.at[col],
            device_id=(row, o), device_id_type=MESH)

    @pl.loop(0, 16)
    def _(u):
        t = rem(u + 8, 16)
        o = rem(col + t, 16)
        for slot in range(2):
            stage[t, slot] = (total[owned_m[2 * o + slot]] * owned_f[2 * o + slot]).astype(BF16)

        @pl.when(t != 0)
        def _():
            out_copy(t).start()

        @pl.when(t == 0)
        def _():
            pltpu.make_async_copy(stage.at[0], out.at[col], own_sem).start()

    pltpu.make_async_copy(stage.at[0], out.at[col], own_sem).wait()

    @pl.loop(1, 16)
    def _(t):
        meta_a_copy(t).wait_send()
        out_copy(t).wait_send()

    @pl.loop(1, 8)
    def _(t):
        meta_b_copy(t).wait_send()

    for number in range(len(COPIES)):
        copy_of(number).wait_send()

    @pl.loop(1, 16)
    def _(t):
        source = rem(col + t, 16)
        pltpu.make_async_remote_copy(
            src_ref=stage.at[t], dst_ref=out.at[source], send_sem=out_send.at[t], recv_sem=out_recv.at[source],
            device_id=(row, source), device_id_type=MESH).wait_recv()


def on_device(a_blocks, a_rows, b_blocks, b_cols, screen, keep, owners):
    vmem, smem = pl.BlockSpec(memory_space=pltpu.VMEM), pl.BlockSpec(memory_space=pltpu.SMEM)
    dma = pltpu.SemaphoreType.DMA
    out = pl.pallas_call(
        kernel,
        out_shape=jax.ShapeDtypeStruct((16, 2, W, W), BF16),
        in_specs=[vmem, vmem, smem, smem, smem, smem, smem],
        out_specs=pl.BlockSpec(memory_space=pl.ANY),
        scratch_shapes=[
            pltpu.VMEM((16, 28, W, W), BF16),
            pltpu.VMEM((8, 24, W, W), BF16),
            pltpu.VMEM((32, W, W), F32),
            pltpu.VMEM((8 * W, 2 * W), BF16),
            pltpu.VMEM((16, 2, W, W), BF16),
            pltpu.SMEM((W,), I32),
            pltpu.SMEM((2048,), F32),
            pltpu.SMEM((16, W), I32),
            pltpu.SMEM((8, W), I32),
            pltpu.SMEM((32,), I32),
            pltpu.SMEM((32,), F32),
            dma((16 * len(A_PIECES),)),
            dma((8 * len(B_PIECES),)),
            dma((len(COPIES),)),
            dma((16,)),
            dma((16,)),
            dma((8,)),
            dma((8,)),
            dma((16,)),
            dma((16,)),
            dma,
        ],
        compiler_params=pltpu.CompilerParams(
            collective_id=0, has_side_effects=True, vmem_limit_bytes=48 * 2**20),
        cost_estimate=pl.CostEstimate(flops=8_600_000_000, bytes_accessed=4_000_000, transcendentals=0),
        name="gather_multiply_send",
    )(
        a_blocks[0, 0], b_blocks[0, 0].reshape(8, 3, W, W), a_rows[0, 0], jnp.transpose(b_cols[0, 0], (2, 0, 1)),
        jnp.transpose(screen[0, 0], (2, 3, 1, 0)), keep[0, 0], owners[0, 0, :, 0],
    )
    return out[None, None]


def solution(mesh):
    in_specs = (
        P("row", "col", None, None, None, None),
        P("row", "col", None, None),
        P("row", "col", None, None, None, None, None),
        P("row", "col", None, None, None),
        P("row", "col", None, None, None, None),
        P("row", "col", None),
        P("row", "col", None, None),
    )
    out_specs = P("row", "col", None, None, None, None)
    return jax.shard_map(
        on_device, mesh=mesh, in_specs=in_specs, out_specs=out_specs, check_vma=False
    )
```

time: 590 us -> 132 us (0.22); the launches traced: 584 us -> 132 us
  waiting for transfers between devices: 232 us -> 0 us
  starting transfers between devices: 154 us -> 0 us
  Pallas kernels: 0 us -> 127 us
  local copies, waits for them, and re-layouts: 71 us -> 4.77 us
  matrix products: 62.6 us -> 0 us
  other arithmetic: 42.9 us -> 0 us
  blocking collectives: 20.2 us -> 0 us
    ppermute x60 -> x0, waiting for transfers between devices: 232 us -> none  [passed_along(): return lax.ppermute(block, axis, route)]
    ppermute x60 -> x0, starting transfers between devices: 154 us -> none  [passed_along(): return lax.ppermute(block, axis, route)]
    pallas_call x0 -> x1, Pallas kernels: none -> 127 us  [on_device(): pl.pallas_call(kernel, out_shape=jax.ShapeDtypeStruct((16, 2, W, W), BF16...]
    dot_general x49 -> x0, matrix products: 62.6 us -> none  [the longest x16 29.3 us: tile_product(): jnp.einsum('kcrxy,kcyz->rcxz', a_chosen, b_chosen, preferred_element_type...]
    while x76 -> x0, local copies, waits for them, and re-layouts: 61.3 us -> none
    select_n x30 -> x0, other arithmetic: 38.3 us -> none  [the longest x15 38.2 us: advance(): b_pair = jnp.where(last_row, b_pair[::-1], b_pair)]
    all_to_all x1 -> x0, blocking collectives: 20.2 us -> none  [on_device(): lax.all_to_all(outgoing[None, None], 'col', split_axis=2, concat_axis=2,...]
  transfers between devices with their start and end apart: 60 -> 0, of which waited for: 17 -> 0; matrix products, arithmetic and copies ran while one was open for 28% -> 0% of each run, Pallas kernels for 0% -> 0%
where the time goes in v1:
time: 132 us
  Pallas kernels  127 us (96%)
  local copies, waits for them, and re-layouts  4.77 us (4%)
    pallas_call x1, Pallas kernels, on_device(): pl.pallas_call(kernel, out_shape=jax.ShapeDtypeStruct((16, 2, W, W), BF16...  127 us
    unnamed x15, local copies, waits for them, and re-layouts  4.77 us

profile of v1, /device:TPU:1, one launch (start us, length us, event | category | flops | bytes accessed | tf_op | source)
XLA Modules:
  0.0 132.1 jit_solution(462683115544362194)
XLA Ops:
  0.0 0.0 copy-start.6
  0.0 0.0 copy-start.3
  0.0 0.0 copy-start.4
  0.0 0.0 copy-start.5
  0.0 0.6 copy-done.6
  0.7 0.0 copy-done.3
  0.7 0.0 copy-done.4
  0.7 0.0 copy-done.5
  0.7 0.0 copy-start
  0.7 1.2 copy-done
  1.9 0.0 copy-start.1
  1.9 1.1 copy-done.1
  3.0 0.0 copy-start.2
  3.0 0.8 copy-done.2
  3.8 127.3 %gather_multiply_send.1 = bf16[16,2,128,128]{3,2,1,0:T(8,128)(2,1)S(1)} custom-call(bf16[4,7,128,128]{3,2,1,0:T(8,128)(2,1)S(1)} %bitcast.13, bf16[8,3,128,128]{3,2,1,0:T(8,128)(2,1)S(1)} %bitcast.14, s32[4,7]{1,0:T(4,128)S(1)} %bitcast.17, s32[3,2,4]{2,1,0:T(2,128)S(1)} %bitcast.16, s32[7,3,4,16]{3,2,1,0:T(4,128)S(1)} %bitcast.15, s32[32]{0:T(128)S(1)} %bitcast.18, ...), custom_call_target="tpu_custom_call" | custom-call | flops 8600000512 | bytes 4000000 | tf_op jit(solution)/shard_map/gather_multiply_send/pallas_call | solution.py:412
  131.2 1.0 copy.9
Async XLA Ops:
  0.0 0.7 copy-start.6
  0.0 0.7 copy-start.3
  0.0 0.7 copy-start.4
  0.0 0.7 copy-start.5
  0.7 1.2 copy-start
  1.9 1.1 copy-start.1
  3.0 0.8 copy-start.2

commit v2 on v1

--- a/solution.py
+++ b/solution.py
@@ -14,7 +14,6 @@
 A_PIECES = ((0, 7), (7, 7), (14, 4), (18, 3), (21, 7))
 B_PIECES = ((0, 6), (6, 6), (12, 6), (18, 6))
 A_HALF = ((0, 1), (2, 3, 4))
-UNIT = 0.624
 
 
 def a_slot(dy, dz, dk):
@@ -60,41 +59,39 @@
     return []
 
 
-def arrivals():
-    ends = [lo + n for lo, n in A_PIECES]
-    out = []
-
-    def a(dy, dz, p, t):
-        out.append((t, "A", a_slot(dy, dz, 0), p))
-        out.append((t + 2.0, "A", a_slot(dy, dz, 1), p))
-
-    for p in range(5):
-        out.append((1.5 + ends[p] * 0.1, "A", a_slot(0, 0, 1), p))
-        a(1, 0, p, UNIT * ends[p])
-        a(3, 0, p, UNIT * ends[p])
-        a(0, 1, p, 2 * UNIT * ends[p] * 0.92)
-        a(2, 0, p, UNIT * (28 + (ends[p] if p < 2 else ends[p] - 14)))
-        if p:
-            a(1, 1, p, UNIT * (42 + ends[p] - 7))
-            a(3, 1, p, UNIT * (42 + ends[p] - 7))
-            a(2, 1, p, UNIT * (63 + (ends[p] - 7 if p < 3 else ends[p] - 18)))
-    a(1, 1, 0, UNIT * 58)
-    a(3, 1, 0, UNIT * 60)
-    a(2, 1, 0, UNIT * 70)
-    for c in range(4):
-        e = 6 * (c + 1)
-        half = 6 * (c % 2 + 1)
-        for dx in (1, 3):
-            out.append((UNIT * e, "B", b_slot(dx, 0), c))
-            out.append((UNIT * (36 + e), "B", b_slot(dx, 1), c))
-        out.append((2 * UNIT * e, "B", b_slot(0, 1), c))
-        out.append((UNIT * (24 + half), "B", b_slot(2, 0), c))
-        out.append((UNIT * (60 + half), "B", b_slot(2, 1), c))
-    return sorted(out, key=lambda r: r[0])
-
-
-def make_plan(step):
-    phases, copies = [[]], []
+ORDER = (
+    ((0, 1, 0), (0, 1, 1), (0, 1, 2), (1, 2, 0), (1, 6, 0), (0, 1, 3),),
+    ((0, 1, 4), (0, 4, 0), (0, 12, 0),),
+    ((1, 1, 0), (1, 2, 1), (1, 6, 1), (0, 13, 0),),
+    ((0, 2, 0), (0, 5, 0), (0, 4, 1), (0, 12, 1),),
+    ((0, 4, 2), (0, 12, 2), (1, 2, 2), (1, 6, 2),),
+    ((0, 3, 0), (0, 13, 1), (0, 4, 3), (0, 12, 3), (0, 5, 1),),
+    ((1, 1, 1), (0, 13, 2), (1, 2, 3), (1, 6, 3), (0, 5, 2),),
+    ((0, 13, 3), (0, 5, 3), (0, 2, 1), (0, 4, 4), (0, 12, 4),),
+    ((1, 3, 0), (1, 4, 0),),
+    ((0, 8, 2),),
+    ((0, 3, 1), (0, 13, 4), (0, 8, 0), (0, 8, 3), (0, 5, 4), (1, 1, 2),),
+    ((0, 2, 2), (1, 4, 2), (1, 7, 0),),
+    ((0, 9, 2),),
+    ((0, 9, 0), (0, 9, 3), (0, 2, 3), (0, 3, 2), (0, 6, 1), (0, 8, 1), (1, 3, 1), (1, 4, 1),),
+    ((1, 1, 3), (0, 3, 3), (1, 4, 3), (1, 7, 1), (0, 9, 1), (0, 8, 4), (0, 14, 1), (0, 7, 1),),
+    ((0, 2, 4), (0, 6, 2), (0, 14, 2),),
+    ((1, 3, 2), (1, 7, 2), (0, 15, 1),),
+    ((0, 6, 3), (0, 14, 3), (0, 9, 4),),
+    ((0, 3, 4), (0, 14, 0), (0, 15, 2), (0, 7, 2),),
+    ((1, 3, 3), (1, 5, 0),),
+    ((0, 15, 3), (0, 7, 3), (0, 6, 4), (0, 10, 1),),
+    ((0, 15, 0), (0, 6, 0), (0, 10, 3), (1, 5, 2), (1, 7, 3),),
+    ((0, 11, 1), (0, 14, 4), (0, 7, 4),),
+    ((1, 5, 1), (1, 5, 3), (0, 7, 0), (0, 11, 3), (0, 10, 0), (0, 10, 4),),
+    ((0, 10, 2),),
+    ((0, 15, 4),),
+    ((0, 11, 0), (0, 11, 4), (0, 11, 2),),
+)
+
+
+def make_plan():
+    phases, copies = [[]] + [[("AB"[kind], slot, piece) for kind, slot, piece in phase] for phase in ORDER], []
 
     def start(kind, slot, piece, phase):
         if kind == "A":
@@ -109,15 +106,9 @@
         start("A", 0, p, 0)
         if p < 4:
             start("B", 0, p, 0)
-    last = 0.0
-    for t, kind, slot, piece in arrivals():
-        if t - last > step or not phases[-1]:
-            if phases[-1]:
-                last = t
-            phases.append([])
-            last = t
-        phases[-1].append((kind, slot, piece))
-        start(kind, slot, piece, len(phases) - 1)
+    for n, phase in enumerate(phases):
+        for kind, slot, piece in phase:
+            start(kind, slot, piece, n)
     when_a = [0] * 32
     when_b = [0] * 32
     for n, phase in enumerate(phases):
@@ -136,7 +127,7 @@
     return phases, copies, when_a, when_b, triggers, bounds
 
 
-PHASES, COPIES, WHEN_A, WHEN_B, TRIGGERS, BOUNDS = make_plan(2.4)
+PHASES, COPIES, WHEN_A, WHEN_B, TRIGGERS, BOUNDS = make_plan()
 
 
 def entry(table, at):
@@ -148,8 +139,8 @@
     return lax.rem(lax.shift_right_logical(word, 7 * lax.rem(at, 4)), 128)
 
 
-def kernel(a_in, b_in, a_rows, b_cols, screen, keep, owners, out, a_all, b_all, total, dense, stage, lists, mask, meta_a,
-           meta_b, owned_m, owned_f, a_recv, b_recv, sent, ma_send, ma_recv, mb_send, mb_recv, out_send, out_recv, own_sem):
+def kernel(a_hbm, b_hbm, a_rows, b_cols, screen, keep, owners, out, a_in, b_in, a_all, b_all, total, dense, stage, lists, meta_a,
+           meta_b, owned_m, owned_f, a_recv, b_recv, sent, ma_send, ma_recv, mb_send, mb_recv, out_send, out_recv, own_sem, in_sem):
     row, col = lax.axis_index("row"), lax.axis_index("col")
     rem, div = lax.rem, lax.div
     x, zh = div(row, 2), rem(row, 2)
@@ -164,6 +155,11 @@
         "zh": (row + 1 - 2 * zh, col),
     }
 
+    load_a = pltpu.make_async_copy(a_hbm, a_in, in_sem.at[0])
+    load_b = pltpu.make_async_copy(b_hbm, b_in, in_sem.at[1])
+    load_a.start()
+    load_b.start()
+
     barrier = pltpu.get_barrier_semaphore()
 
     @pl.loop(1, 16)
@@ -173,47 +169,46 @@
     @pl.loop(1, 8)
     def _(t):
         pl.semaphore_signal(barrier, inc=1, device_id=(rem(row + t, 8), col), device_id_type=MESH)
+
+    def note(at, value):
+        lists[at] = value
+        meta_a[col, at] = value
+        meta_b[row, at] = value
 
     for i in list(range(36, 64)) + list(range(104, W)):
         lists[i] = I32(0)
     for k in range(4):
         gone = I32(28)
-        places = [I32(7)] * 8
+        places = [I32(0)] * 8
         for a in range(7):
             at = a_rows[k, a]
             gone = gone - at
             places = [jnp.where(at == r, a, v) for r, v in enumerate(places)]
         for r in range(8):
-            lists[k * 8 + r] = places[r]
-        lists[32 + k] = gone
+            note(k * 8 + r, places[r])
+        note(32 + k, gone)
     for h in range(2):
         for k in range(4):
             gone = I32(6)
-            places = [I32(3)] * 4
+            places = [I32(0)] * 4
             for b in range(3):
                 at = b_cols[b, h, k]
                 gone = gone - at
                 places = [jnp.where(at == c, b, v) for c, v in enumerate(places)]
             for c in range(4):
-                lists[64 + h * 16 + k * 4 + c] = places[c]
-            lists[96 + h * 4 + k] = gone
-
-    @pl.loop(0, W)
-    def _(i):
-        meta_a[col, i] = lists[i]
-        meta_b[row, i] = lists[i]
-
-    @pl.loop(0, 28)
-    def _(i):
-        k, n = div(i, 7), rem(i, 7)
-        place = n + jnp.where(n >= lists[32 + k], 1, 0)
-        a_all[0, i] = a_in[k, jnp.minimum(lists[k * 8 + place], 6)]
-
-    @pl.loop(0, 24)
-    def _(i):
-        hk, n = div(i, 3), rem(i, 3)
-        place = n + jnp.where(n >= lists[96 + hk], 1, 0)
-        b_all[0, i] = b_in[hk, jnp.minimum(lists[64 + hk * 4 + place], 2)]
+                note(64 + h * 16 + k * 4 + c, places[c])
+            note(96 + h * 4 + k, gone)
+
+    load_a.wait()
+    for k in range(4):
+        gone = lists[32 + k]
+        for n in range(7):
+            a_all[0, k * 7 + n] = a_in[k, lists[k * 8 + n + jnp.where(n >= gone, 1, 0)]]
+    load_b.wait()
+    for hk in range(8):
+        gone = lists[96 + hk]
+        for n in range(3):
+            b_all[0, hk * 3 + n] = b_in[hk, lists[64 + hk * 4 + n + jnp.where(n >= gone, 1, 0)]]
 
     def copy_of(number):
         _, kind, slot, there, piece, target = COPIES[number]
@@ -244,25 +239,17 @@
 
     pl.semaphore_wait(barrier, 22)
 
+    @pl.loop(1, 16)
+    def _(t):
+        meta_a_copy(t).start()
+
+    @pl.loop(1, 8)
+    def _(t):
+        meta_b_copy(t).start()
+
     for number, copy in enumerate(COPIES):
         if copy[0] == 0:
             copy_of(number).start()
-
-    @pl.loop(1, 16)
-    def _(t):
-        meta_a_copy(t).start()
-
-    @pl.loop(1, 8)
-    def _(t):
-        meta_b_copy(t).start()
-
-    @pl.loop(0, 16)
-    def _(s):
-        for k in range(4):
-            for a in range(8):
-                for b in range(4):
-                    at = (s * 4 + k) * 32 + a * 4 + b
-                    mask[at] = screen[a, b, k, s].astype(F32) if a < 7 and b < 3 else F32(0)
 
     @pl.loop(0, 16)
     def _(o):
@@ -304,21 +291,23 @@
             for r in range(8):
                 low = a_all[qa, k * 7 + min(r, 6)]
                 high = a_all[qa, k * 7 + max(r - 1, 0)]
-                dense[r * W:(r + 1) * W, kk * W:(kk + 1) * W] = jnp.where(r < gone, low, high)
+                dense[r * W:(r + 1) * W, kk * W:(kk + 1) * W] = jnp.where(
+                    r == gone, jnp.zeros_like(low), jnp.where(r < gone, low, high))
         for c in range(4):
             right = []
             for kk in range(2):
                 hk = h * 4 + half * 2 + kk
                 low = b_all[qb, hk * 3 + min(c, 2)]
                 high = b_all[qb, hk * 3 + max(c - 1, 0)]
-                right.append(jnp.where(c < meta_b[p, 96 + hk], low, high))
+                gone = meta_b[p, 96 + hk]
+                right.append(jnp.where(c == gone, jnp.zeros_like(low), jnp.where(c < gone, low, high)))
             rows = []
             for r in range(8):
                 cells = []
                 for kk in range(2):
                     k = half * 2 + kk
-                    at = (s * 4 + k) * 32 + meta_a[g, k * 8 + r] * 4 + meta_b[p, 64 + h * 16 + k * 4 + c]
-                    cells.append(dense[r * W:(r + 1) * W, kk * W:(kk + 1) * W] * mask[at].astype(BF16))
+                    passed = screen[meta_a[g, k * 8 + r], meta_b[p, 64 + h * 16 + k * 4 + c], k, s].astype(F32)
+                    cells.append(dense[r * W:(r + 1) * W, kk * W:(kk + 1) * W] * passed.astype(BF16))
                 rows.append(jnp.concatenate(cells, axis=1))
             left = jnp.concatenate(rows, axis=0)
             part = jnp.dot(left, jnp.concatenate(right, axis=0), preferred_element_type=F32)
@@ -407,21 +396,22 @@
 
 
 def on_device(a_blocks, a_rows, b_blocks, b_cols, screen, keep, owners):
-    vmem, smem = pl.BlockSpec(memory_space=pltpu.VMEM), pl.BlockSpec(memory_space=pltpu.SMEM)
+    hbm, smem = pl.BlockSpec(memory_space=pl.ANY), pl.BlockSpec(memory_space=pltpu.SMEM)
     dma = pltpu.SemaphoreType.DMA
     out = pl.pallas_call(
         kernel,
         out_shape=jax.ShapeDtypeStruct((16, 2, W, W), BF16),
-        in_specs=[vmem, vmem, smem, smem, smem, smem, smem],
-        out_specs=pl.BlockSpec(memory_space=pl.ANY),
+        in_specs=[hbm, hbm, smem, smem, smem, smem, smem],
+        out_specs=hbm,
         scratch_shapes=[
+            pltpu.VMEM((4, 7, W, W), BF16),
+            pltpu.VMEM((8, 3, W, W), BF16),
             pltpu.VMEM((16, 28, W, W), BF16),
             pltpu.VMEM((8, 24, W, W), BF16),
             pltpu.VMEM((32, W, W), F32),
             pltpu.VMEM((8 * W, 2 * W), BF16),
             pltpu.VMEM((16, 2, W, W), BF16),
             pltpu.SMEM((W,), I32),
-            pltpu.SMEM((2048,), F32),
             pltpu.SMEM((16, W), I32),
             pltpu.SMEM((8, W), I32),
             pltpu.SMEM((32,), I32),
@@ -436,9 +426,10 @@
             dma((16,)),
             dma((16,)),
             dma,
+            dma((2,)),
         ],
         compiler_params=pltpu.CompilerParams(
-            collective_id=0, has_side_effects=True, vmem_limit_bytes=48 * 2**20),
+            collective_id=0, has_side_effects=True, vmem_limit_bytes=60 * 2**20),
         cost_estimate=pl.CostEstimate(flops=8_600_000_000, bytes_accessed=4_000_000, transcendentals=0),
         name="gather_multiply_send",
     )(

time: 132 us -> 97.4 us (0.74)
  Pallas kernels: 127 us -> 94.8 us
  local copies, waits for them, and re-layouts: 4.77 us -> 2.31 us
    pallas_call x1, Pallas kernels: 127 us -> 94.8 us  [on_device(): pl.pallas_call(kernel, out_shape=jax.ShapeDtypeStruct((16, 2, W, W), BF16...]
    unnamed x15 -> x1, local copies, waits for them, and re-layouts: 4.77 us -> 2.31 us
where the time goes in v2:
time: 97.4 us; the launch traced here: 97.1 us
  Pallas kernels  94.8 us (97%)
  local copies, waits for them, and re-layouts  2.31 us (2%)
    pallas_call x1, Pallas kernels, on_device(): pl.pallas_call(kernel, out_shape=jax.ShapeDtypeStruct((16, 2, W, W), BF16...  94.8 us
    unnamed x1, local copies, waits for them, and re-layouts  2.31 us

profile of v2, /device:TPU:1, one launch (start us, length us, event | category | flops | bytes accessed | tf_op | source)
XLA Modules:
  0.0 97.1 jit_solution(6220234555327473947)
XLA Ops:
  0.0 94.8 %gather_multiply_send.1 = bf16[16,2,128,128]{3,2,1,0:T(8,128)(2,1)} custom-call(bf16[4,7,128,128]{3,2,1,0:T(8,128)(2,1)} %bitcast.13, bf16[8,3,128,128]{3,2,1,0:T(8,128)(2,1)} %bitcast.14, s32[4,7]{1,0:T(4,128)} %bitcast.17, s32[3,2,4]{2,1,0:T(2,128)} %bitcast.16, s32[7,3,4,16]{3,2,1,0:T(4,128)} %bitcast.15, s32[32]{0:T(128)} %bitcast.18, s32[32]{0:T(128)} %bitcast.19), custom_call_target="tpu_custom_call" | custom-call | flops 8600000512 | bytes 4000000 | tf_op jit(solution)/shard_map/gather_multiply_send/pallas_call | solution.py:401
  94.8 2.3 %copy.9 = bf16[1,1,16,2,128,128]{5,4,3,2,1,0:T(8,128)(2,1)} copy(bf16[1,1,16,2,128,128]{5,4,3,2,1,0:T(8,128)(2,1)} %bitcast.12) | data formatting | bytes 2097152

commit v3 on v2

--- a/solution.py
+++ b/solution.py
@@ -11,132 +11,66 @@
 BF16, F32, I32 = jnp.bfloat16, jnp.float32, jnp.int32
 W = 128
 
-A_PIECES = ((0, 7), (7, 7), (14, 4), (18, 3), (21, 7))
+A_PIECES = ((0, 4), (4, 5), (9, 5), (14, 3), (17, 5), (22, 6))
 B_PIECES = ((0, 6), (6, 6), (12, 6), (18, 6))
-A_HALF = ((0, 1), (2, 3, 4))
-
-
-def a_slot(dy, dz, dk):
-    return (dy % 4) * 4 + dz * 2 + dk
-
-
-def b_slot(dx, dz):
-    return (dx % 4) * 2 + dz
-
-
-def a_forwards(dy, dz, p):
-    out = []
-    if (dy, dz) == (0, 0):
-        out += [("y+", a_slot(3, 0, 0)), ("y-", a_slot(1, 0, 0)), ("zl", a_slot(0, 1, 0))]
-    elif (dy, dz) == (0, 1):
-        if p >= 1:
-            out += [("y+", a_slot(3, 1, 0)), ("y-", a_slot(1, 1, 0))]
-    elif dz == 0:
-        if dy == 3 and p in (0, 1):
-            out.append(("y+", a_slot(2, 0, 0)))
-        if dy == 1 and p in (2, 3, 4):
-            out.append(("y-", a_slot(2, 0, 0)))
-        if p == 0:
-            out.append(("zl", a_slot(dy, 1, 0)))
-    else:
-        if dy == 3 and p in (1, 2):
-            out.append(("y+", a_slot(2, 1, 0)))
-        if dy == 1 and p in (3, 4):
-            out.append(("y-", a_slot(2, 1, 0)))
-    out.append(("sib", a_slot(dy, dz, 1)))
-    return out
-
-
-def b_forwards(dx, dz, c):
-    if (dx, dz) == (0, 0):
-        return [("x+", b_slot(3, 0)), ("x-", b_slot(1, 0)), ("zh", b_slot(0, 1))]
-    if dx == 0:
-        return [("x+", b_slot(3, 1)), ("x-", b_slot(1, 1))]
-    if dx == 3 and c in (0, 1):
-        return [("x+", b_slot(2, dz))]
-    if dx == 1 and c in (2, 3):
-        return [("x-", b_slot(2, dz))]
-    return []
-
-
+A_HALF = tuple(lo // 14 for lo, _ in A_PIECES)
 ORDER = (
-    ((0, 1, 0), (0, 1, 1), (0, 1, 2), (1, 2, 0), (1, 6, 0), (0, 1, 3),),
-    ((0, 1, 4), (0, 4, 0), (0, 12, 0),),
-    ((1, 1, 0), (1, 2, 1), (1, 6, 1), (0, 13, 0),),
-    ((0, 2, 0), (0, 5, 0), (0, 4, 1), (0, 12, 1),),
-    ((0, 4, 2), (0, 12, 2), (1, 2, 2), (1, 6, 2),),
-    ((0, 3, 0), (0, 13, 1), (0, 4, 3), (0, 12, 3), (0, 5, 1),),
-    ((1, 1, 1), (0, 13, 2), (1, 2, 3), (1, 6, 3), (0, 5, 2),),
-    ((0, 13, 3), (0, 5, 3), (0, 2, 1), (0, 4, 4), (0, 12, 4),),
-    ((1, 3, 0), (1, 4, 0),),
-    ((0, 8, 2),),
-    ((0, 3, 1), (0, 13, 4), (0, 8, 0), (0, 8, 3), (0, 5, 4), (1, 1, 2),),
-    ((0, 2, 2), (1, 4, 2), (1, 7, 0),),
-    ((0, 9, 2),),
-    ((0, 9, 0), (0, 9, 3), (0, 2, 3), (0, 3, 2), (0, 6, 1), (0, 8, 1), (1, 3, 1), (1, 4, 1),),
-    ((1, 1, 3), (0, 3, 3), (1, 4, 3), (1, 7, 1), (0, 9, 1), (0, 8, 4), (0, 14, 1), (0, 7, 1),),
-    ((0, 2, 4), (0, 6, 2), (0, 14, 2),),
-    ((1, 3, 2), (1, 7, 2), (0, 15, 1),),
-    ((0, 6, 3), (0, 14, 3), (0, 9, 4),),
-    ((0, 3, 4), (0, 14, 0), (0, 15, 2), (0, 7, 2),),
-    ((1, 3, 3), (1, 5, 0),),
-    ((0, 15, 3), (0, 7, 3), (0, 6, 4), (0, 10, 1),),
-    ((0, 15, 0), (0, 6, 0), (0, 10, 3), (1, 5, 2), (1, 7, 3),),
-    ((0, 11, 1), (0, 14, 4), (0, 7, 4),),
-    ((1, 5, 1), (1, 5, 3), (0, 7, 0), (0, 11, 3), (0, 10, 0), (0, 10, 4),),
-    ((0, 10, 2),),
-    ((0, 15, 4),),
-    ((0, 11, 0), (0, 11, 4), (0, 11, 2),),
+    (0, 2, 0), (0, 4, 0), (0, 12, 0), (1, 2, 0), (1, 6, 0), (0, 1, 0), (0, 1, 1), (0, 1, 2), (0, 1, 3), (0, 1, 4),
+    (0, 1, 5), (0, 4, 1), (0, 12, 1), (1, 1, 0), (1, 2, 2), (1, 6, 2), (0, 13, 0), (0, 5, 0), (0, 3, 0), (0, 4, 2),
+    (0, 12, 2), (0, 2, 1), (0, 4, 3), (0, 13, 1), (0, 8, 0), (1, 4, 0), (0, 5, 1), (1, 3, 0), (0, 12, 3), (1, 1, 2),
+    (0, 8, 2), (0, 13, 2), (0, 5, 2), (0, 3, 1), (1, 7, 0), (1, 2, 1), (0, 5, 3), (0, 2, 2), (0, 8, 1), (0, 9, 0),
+    (0, 6, 1), (0, 13, 3), (0, 14, 0), (1, 6, 1), (1, 2, 3), (0, 9, 2), (0, 14, 1), (0, 4, 4), (0, 2, 3), (0, 9, 1),
+    (0, 8, 3), (0, 3, 2), (0, 7, 1), (0, 12, 4), (1, 6, 3), (1, 4, 2), (0, 6, 0), (0, 15, 0), (0, 15, 1), (0, 6, 2),
+    (0, 5, 4), (0, 14, 2), (0, 3, 3), (1, 7, 2), (1, 3, 2), (1, 1, 1), (0, 9, 3), (0, 13, 4), (0, 7, 0), (0, 4, 5),
+    (0, 12, 5), (1, 5, 0), (1, 4, 3), (0, 7, 2), (1, 1, 3), (0, 15, 2), (0, 10, 2), (0, 10, 1), (0, 2, 4), (1, 4, 1),
+    (1, 5, 2), (0, 5, 5), (0, 13, 5), (0, 8, 4), (0, 8, 5), (0, 2, 5), (1, 7, 1), (0, 11, 2), (1, 3, 1), (0, 11, 1),
+    (0, 6, 4), (0, 14, 4), (0, 6, 3), (0, 3, 4), (1, 7, 3), (0, 9, 4), (0, 9, 5), (1, 3, 3), (0, 10, 0), (0, 6, 5),
+    (0, 14, 5), (0, 3, 5), (0, 14, 3), (0, 15, 4), (0, 7, 4), (0, 7, 3), (1, 5, 1), (0, 10, 3), (0, 10, 4), (1, 5, 3),
+    (0, 11, 0), (0, 10, 5), (0, 15, 5), (0, 7, 5), (0, 15, 3), (0, 11, 3), (0, 11, 4), (0, 11, 5),
 )
+COPIES = (
+    (0, 0, 0, 12, 0, 0), (0, 0, 0, 4, 0, 1), (0, 0, 0, 2, 0, 2), (0, 0, 0, 1, 0, 6), (0, 1, 0, 6, 0, 3), (0, 1, 0, 2, 0, 4),
+    (0, 1, 0, 1, 0, 5), (0, 0, 0, 12, 1, 0), (0, 0, 0, 4, 1, 1), (0, 0, 0, 2, 1, 2), (0, 0, 0, 1, 1, 6), (0, 1, 0, 6, 2, 3),
+    (0, 1, 0, 2, 2, 4), (0, 1, 0, 1, 2, 5), (0, 0, 0, 12, 2, 0), (0, 0, 0, 4, 2, 1), (0, 0, 0, 2, 2, 2), (0, 0, 0, 1, 2, 6),
+    (0, 0, 0, 1, 3, 6), (0, 0, 0, 1, 4, 6), (0, 0, 0, 1, 5, 6), (1, 0, 2, 3, 0, 6), (1, 0, 0, 12, 3, 0), (1, 0, 0, 4, 3, 1),
+    (2, 0, 4, 6, 0, 2), (2, 0, 4, 5, 0, 6), (3, 0, 12, 8, 0, 0), (3, 0, 12, 14, 0, 2), (3, 0, 12, 13, 0, 6), (3, 0, 0, 2, 3, 2),
+    (5, 1, 6, 4, 0, 3), (5, 1, 0, 1, 1, 5), (5, 1, 0, 1, 3, 5), (12, 0, 4, 5, 1, 6), (13, 0, 12, 8, 1, 0), (13, 0, 12, 13, 1, 6),
+    (13, 0, 0, 2, 4, 2), (14, 1, 1, 7, 0, 3), (14, 1, 1, 3, 0, 4), (14, 1, 0, 6, 1, 3), (14, 1, 0, 2, 1, 4), (14, 1, 0, 6, 3, 3),
+    (14, 1, 0, 2, 3, 4), (15, 1, 2, 4, 2, 4), (20, 0, 4, 8, 2, 1), (20, 0, 4, 5, 2, 6), (21, 0, 12, 13, 2, 6), (21, 0, 0, 2, 5, 2),
+    (22, 0, 2, 14, 1, 0), (22, 0, 2, 6, 1, 1), (22, 0, 2, 3, 1, 6), (22, 0, 0, 12, 4, 0), (22, 0, 0, 4, 4, 1), (23, 0, 4, 8, 3, 1),
+    (23, 0, 4, 6, 3, 2), (23, 0, 4, 5, 3, 6), (25, 0, 8, 10, 0, 2), (25, 0, 8, 9, 0, 6), (29, 0, 12, 14, 3, 2), (29, 0, 12, 13, 3, 6),
+    (30, 1, 1, 7, 2, 3), (30, 1, 1, 3, 2, 4), (31, 0, 8, 9, 2, 6), (35, 1, 7, 5, 0, 3), (38, 0, 2, 14, 2, 0), (38, 0, 2, 6, 2, 1),
+    (38, 0, 2, 3, 2, 6), (38, 0, 0, 12, 5, 0), (38, 0, 0, 4, 5, 1), (39, 0, 8, 9, 1, 6), (41, 0, 6, 7, 1, 6), (43, 0, 14, 15, 0, 6),
+    (44, 1, 6, 4, 1, 3), (45, 1, 2, 4, 3, 4), (47, 0, 14, 10, 1, 0), (47, 0, 14, 15, 1, 6), (48, 0, 4, 5, 4, 6), (49, 0, 2, 3, 3, 6),
+    (51, 0, 8, 10, 3, 2), (51, 0, 8, 9, 3, 6), (54, 0, 12, 8, 4, 0), (54, 0, 12, 13, 4, 6), (57, 0, 6, 7, 0, 6), (60, 0, 6, 10, 2, 1),
+    (60, 0, 6, 7, 2, 6), (62, 0, 14, 15, 2, 6), (65, 1, 3, 5, 2, 4), (66, 1, 1, 7, 1, 3), (66, 1, 1, 3, 1, 4), (70, 0, 4, 8, 5, 1),
+    (70, 0, 4, 5, 5, 6), (71, 0, 12, 13, 5, 6), (75, 1, 1, 7, 3, 3), (75, 1, 1, 3, 3, 4), (77, 0, 10, 11, 2, 6), (78, 0, 10, 11, 1, 6),
+    (79, 0, 2, 14, 4, 0), (79, 0, 2, 6, 4, 1), (79, 0, 2, 3, 4, 6), (84, 0, 8, 9, 4, 6), (85, 0, 8, 9, 5, 6), (86, 0, 2, 14, 5, 0),
+    (86, 0, 2, 6, 5, 1), (86, 0, 2, 3, 5, 6), (87, 1, 7, 5, 1, 3), (91, 0, 6, 7, 4, 6), (92, 0, 14, 10, 4, 0), (92, 0, 14, 15, 4, 6),
+    (93, 0, 6, 7, 3, 6), (98, 1, 3, 5, 3, 4), (99, 0, 10, 11, 0, 6), (100, 0, 6, 10, 5, 1), (100, 0, 6, 7, 5, 6), (101, 0, 14, 15, 5, 6),
+    (103, 0, 14, 15, 3, 6), (108, 0, 10, 11, 3, 6), (109, 0, 10, 11, 4, 6), (112, 0, 10, 11, 5, 6),
+)
+TARGETS = ("y+", "y-", "zl", "x+", "x-", "zh", "sib")
 
 
 def make_plan():
-    phases, copies = [[]] + [[("AB"[kind], slot, piece) for kind, slot, piece in phase] for phase in ORDER], []
-
-    def start(kind, slot, piece, phase):
-        if kind == "A":
-            dy, dz, dk = slot // 4, slot // 2 % 2, slot % 2
-            nexts = [] if dk else a_forwards(dy, dz, piece)
+    when_a, when_b, triggers = [0] * 32, [0] * 32, [NOTHING] * (len(ORDER) + 1)
+    for n, (kind, slot, piece) in enumerate(ORDER, 1):
+        if kind == 0:
+            when_a[slot * 2 + A_HALF[piece]] = n
         else:
-            nexts = b_forwards(slot // 2, slot % 2, piece)
-        for target, there in nexts:
-            copies.append((phase, kind, slot, there, piece, target))
-
-    for p in range(5):
-        start("A", 0, p, 0)
-        if p < 4:
-            start("B", 0, p, 0)
-    for n, phase in enumerate(phases):
-        for kind, slot, piece in phase:
-            start(kind, slot, piece, n)
-    when_a = [0] * 32
-    when_b = [0] * 32
-    for n, phase in enumerate(phases):
-        for kind, slot, piece in phase:
-            if kind == "A":
-                at = slot * 2 + (0 if piece in A_HALF[0] else 1)
-                when_a[at] = max(when_a[at], n)
-            else:
-                at = slot * 4 + piece
-                when_b[at] = max(when_b[at], n)
-    triggers, bounds = [], [0]
-    for n in range(len(phases)):
-        triggers += [i for i in range(32) if when_a[i] == n]
-        triggers += [32 + i for i in range(32) if when_b[i] == n]
-        bounds.append(len(triggers))
-    return phases, copies, when_a, when_b, triggers, bounds
-
-
-PHASES, COPIES, WHEN_A, WHEN_B, TRIGGERS, BOUNDS = make_plan()
-
-
-def entry(table, at):
-    padded = list(table) + [0] * (-len(table) % 4)
-    words = [sum(v << (7 * i) for i, v in enumerate(padded[w:w + 4])) for w in range(0, len(padded), 4)]
-    which, word = lax.div(at, 4), I32(words[0])
-    for i, v in enumerate(words[1:], 1):
-        word = jnp.where(which == i, I32(v), word)
-    return lax.rem(lax.shift_right_logical(word, 7 * lax.rem(at, 4)), 128)
+            when_b[slot * 4 + piece] = n
+            triggers[n] = 32 + slot * 4 + piece
+    for at in range(2, 32):
+        triggers[when_a[at]] = at
+    for at in range(2):
+        when_a[at] = triggers.index(NOTHING, 1)
+        triggers[when_a[at]] = at
+    return when_a, when_b, triggers
+
+
+NOTHING = 127
+WHEN_A, WHEN_B, TRIGGERS = make_plan()
 
 
 def kernel(a_hbm, b_hbm, a_rows, b_cols, screen, keep, owners, out, a_in, b_in, a_all, b_all, total, dense, stage, lists, meta_a,
@@ -212,15 +146,15 @@
 
     def copy_of(number):
         _, kind, slot, there, piece, target = COPIES[number]
-        ref, pieces, recv = (a_all, A_PIECES, a_recv) if kind == "A" else (b_all, B_PIECES, b_recv)
+        ref, pieces, recv = (b_all, B_PIECES, b_recv) if kind else (a_all, A_PIECES, a_recv)
         lo, n = pieces[piece]
         return pltpu.make_async_remote_copy(
             src_ref=ref.at[slot, pl.ds(lo, n)], dst_ref=ref.at[there, pl.ds(lo, n)],
             send_sem=sent.at[number], recv_sem=recv.at[there * len(pieces) + piece],
-            device_id=targets[target], device_id_type=MESH)
+            device_id=targets[TARGETS[target]], device_id_type=MESH)
 
     def arrival_of(kind, slot, piece):
-        ref, pieces, recv = (a_all, A_PIECES, a_recv) if kind == "A" else (b_all, B_PIECES, b_recv)
+        ref, pieces, recv = (b_all, B_PIECES, b_recv) if kind else (a_all, A_PIECES, a_recv)
         lo, n = pieces[piece]
         there = ref.at[slot, pl.ds(lo, n)]
         return pltpu.make_async_remote_copy(
@@ -285,72 +219,83 @@
             device_id=(source, col), device_id_type=MESH).wait_recv()
 
     def multiply(qa, half, qb, h, s, g, p):
+        first = half * 14
+        own_rows = [[meta_a[g, half * 16 + kk * 8 + r] for r in range(8)] for kk in range(2)]
+        own_cols = [[meta_b[p, 64 + h * 16 + half * 8 + kk * 4 + c] for c in range(4)] for kk in range(2)]
+        no_row = [meta_a[g, 32 + half * 2 + kk] for kk in range(2)]
+        no_col = [meta_b[p, 96 + h * 4 + half * 2 + kk] for kk in range(2)]
         for kk in range(2):
-            k = half * 2 + kk
-            gone = meta_a[g, 32 + k]
             for r in range(8):
-                low = a_all[qa, k * 7 + min(r, 6)]
-                high = a_all[qa, k * 7 + max(r - 1, 0)]
+                low = a_all[qa, first + kk * 7 + min(r, 6)]
+                high = a_all[qa, first + kk * 7 + max(r - 1, 0)]
                 dense[r * W:(r + 1) * W, kk * W:(kk + 1) * W] = jnp.where(
-                    r == gone, jnp.zeros_like(low), jnp.where(r < gone, low, high))
+                    r == no_row[kk], jnp.zeros_like(low), jnp.where(r < no_row[kk], low, high))
         for c in range(4):
             right = []
             for kk in range(2):
-                hk = h * 4 + half * 2 + kk
-                low = b_all[qb, hk * 3 + min(c, 2)]
-                high = b_all[qb, hk * 3 + max(c - 1, 0)]
-                gone = meta_b[p, 96 + hk]
-                right.append(jnp.where(c == gone, jnp.zeros_like(low), jnp.where(c < gone, low, high)))
+                at = h * 12 + half * 6 + kk * 3
+                low = b_all[qb, at + min(c, 2)]
+                high = b_all[qb, at + max(c - 1, 0)]
+                right.append(jnp.where(
+                    c == no_col[kk], jnp.zeros_like(low), jnp.where(c < no_col[kk], low, high)))
             rows = []
             for r in range(8):
                 cells = []
                 for kk in range(2):
-                    k = half * 2 + kk
-                    passed = screen[meta_a[g, k * 8 + r], meta_b[p, 64 + h * 16 + k * 4 + c], k, s].astype(F32)
+                    passed = screen[own_rows[kk][r], own_cols[kk][c], half * 2 + kk, s].astype(F32)
                     cells.append(dense[r * W:(r + 1) * W, kk * W:(kk + 1) * W] * passed.astype(BF16))
                 rows.append(jnp.concatenate(cells, axis=1))
             left = jnp.concatenate(rows, axis=0)
             part = jnp.dot(left, jnp.concatenate(right, axis=0), preferred_element_type=F32)
             total[c * 8:(c + 1) * 8] += part.reshape(8, W, W)
 
-    @pl.loop(0, len(PHASES))
+    def pair_of(s):
+        g, e = rem(col + s, 16), rem(row + s, 16)
+        p, h = rem(e, 8), div(e, 8)
+        qa = 4 * rem(div(g, 4) - y + 4, 4) + 2 * rem(rem(div(g, 2), 2) + zl, 2) + rem(rem(g, 2) + core, 2)
+        qb = 2 * rem(div(p, 2) - x + 4, 4) + rem(rem(p, 2) + zh, 2)
+        return g, p, h, qa, qb
+
+    def ready_after(n):
+        code = TRIGGERS[n]
+        if code == NOTHING:
+            return I32(-1)
+        half, which = code % 2, code // 2 % 16
+        if code < 32:
+            g = 4 * rem(y + which // 4, 4) + 2 * rem(zl + which // 2 % 2, 2) + rem(core + which % 2, 2)
+            s = rem(g - col + 16, 16)
+            _, _, h, _, qb = pair_of(s)
+            there = [WHEN_B[at * 2 + half] <= n for at in range(16)]
+            at = 2 * qb + h
+        else:
+            p = 2 * rem(x + which // 4, 4) + rem(zh + which // 2 % 2, 2)
+            s = rem(p + 8 * (which % 2) - row + 16, 16)
+            at = pair_of(s)[3]
+            there = [WHEN_A[at * 2 + half] < n for at in range(16)]
+        if not any(there):
+            return I32(-1)
+        both = rem(lax.shift_right_logical(I32(sum(1 << i for i, v in enumerate(there) if v)), at), 2)
+        return jnp.where(both == 1, 2 * s + half, -1)
+
+    def receive(n, low, high):
+        if high - low > 1:
+            middle = (low + high) // 2
+            return lax.cond(n < middle, lambda: receive(n, low, middle), lambda: receive(n, middle, high))
+        arrival_of(*ORDER[low - 1]).wait_recv()
+        for number, copy in enumerate(COPIES):
+            if copy[0] == low:
+                copy_of(number).start()
+        return ready_after(low)
+
+    @pl.loop(1, len(ORDER) + 1)
     def _(n):
-        for i, phase in enumerate(PHASES):
-            if i == 0:
-                continue
-
-            @pl.when(n == i)
-            def _(i=i, phase=phase):
-                for kind, slot, piece in phase:
-                    arrival_of(kind, slot, piece).wait_recv()
-                    for number, copy in enumerate(COPIES):
-                        if copy[0] == i and (copy[1], copy[2], copy[4]) == (kind, slot, piece):
-                            copy_of(number).start()
-
-        @pl.loop(entry(BOUNDS, n), entry(BOUNDS, n + 1))
-        def _(u):
-            code = entry(TRIGGERS, u)
-            by_b = div(code, 32)
-            index = rem(code, 32)
-            half = rem(index, 2)
-            which = div(index, 2)
-            g_a = 4 * rem(y + div(which, 4), 4) + 2 * rem(zl + rem(div(which, 2), 2), 2) + rem(core + rem(which, 2), 2)
-            s_a = rem(g_a - col + 16, 16)
-            p_b = 2 * rem(x + div(which, 4), 4) + rem(zh + rem(div(which, 2), 2), 2)
-            s_b = rem(p_b + 8 * rem(which, 2) - row + 16, 16)
-            s = jnp.where(by_b == 1, s_b, s_a)
-            g = rem(col + s, 16)
-            e = rem(row + s, 16)
-            p, h = rem(e, 8), div(e, 8)
-            qa = 4 * rem(div(g, 4) - y + 4, 4) + 2 * rem(rem(div(g, 2), 2) + zl, 2) + rem(rem(g, 2) + core, 2)
-            qb = 2 * rem(div(p, 2) - x + 4, 4) + rem(rem(p, 2) + zh, 2)
-            when_a = entry(WHEN_A, qa * 2 + half)
-            when_b = entry(WHEN_B, qb * 4 + h * 2 + half)
-            ready = jnp.where(by_b == 1, when_a < n, when_b <= n)
-
-            @pl.when(ready)
-            def _():
-                multiply(qa, half, qb, h, s, g, p)
+        code = receive(n, 1, len(ORDER) + 1)
+
+        @pl.when(code >= 0)
+        def _():
+            s, half = div(code, 2), rem(code, 2)
+            g, p, h, qa, qb = pair_of(s)
+            multiply(qa, half, qb, h, s, g, p)
 
     def out_copy(t):
         o = rem(col + t, 16)

time: 97.4 us -> 90.2 us (0.926)
  Pallas kernels: 94.8 us -> 87.6 us
    pallas_call x1, Pallas kernels: 94.8 us -> 87.6 us  [on_device(): pl.pallas_call(kernel, out_shape=jax.ShapeDtypeStruct((16, 2, W, W), BF16...]
where the time goes in v3:
time: 90.2 us; the launch traced here: 89.9 us
  Pallas kernels  87.6 us (97%)
  local copies, waits for them, and re-layouts  2.31 us (3%)
    pallas_call x1, Pallas kernels, on_device(): pl.pallas_call(kernel, out_shape=jax.ShapeDtypeStruct((16, 2, W, W), BF16...  87.6 us
    unnamed x1, local copies, waits for them, and re-layouts  2.31 us

profile of v3, /device:TPU:1, one launch (start us, length us, event | category | flops | bytes accessed | tf_op | source)
XLA Modules:
  0.0 89.9 jit_solution(15847283743134622926)
XLA Ops:
  0.0 87.6 %gather_multiply_send.1 = bf16[16,2,128,128]{3,2,1,0:T(8,128)(2,1)} custom-call(bf16[4,7,128,128]{3,2,1,0:T(8,128)(2,1)} %bitcast.13, bf16[8,3,128,128]{3,2,1,0:T(8,128)(2,1)} %bitcast.14, s32[4,7]{1,0:T(4,128)} %bitcast.17, s32[3,2,4]{2,1,0:T(2,128)} %bitcast.16, s32[7,3,4,16]{3,2,1,0:T(4,128)} %bitcast.15, s32[32]{0:T(128)} %bitcast.18, s32[32]{0:T(128)} %bitcast.19), custom_call_target="tpu_custom_call" | custom-call | flops 8600000512 | bytes 4000000 | tf_op jit(solution)/shard_map/gather_multiply_send/pallas_call | solution.py:346
  87.6 2.3 %copy.9 = bf16[1,1,16,2,128,128]{5,4,3,2,1,0:T(8,128)(2,1)} copy(bf16[1,1,16,2,128,128]{5,4,3,2,1,0:T(8,128)(2,1)} %bitcast.12) | data formatting | bytes 2097152

commit v4 on v3

--- a/solution.py
+++ b/solution.py
@@ -11,44 +11,36 @@
 BF16, F32, I32 = jnp.bfloat16, jnp.float32, jnp.int32
 W = 128
 
-A_PIECES = ((0, 4), (4, 5), (9, 5), (14, 3), (17, 5), (22, 6))
+A_PIECES = ((0, 4), (4, 5), (9, 5), (14, 3), (17, 5), (22, 6), (0, 14), (14, 14))
 B_PIECES = ((0, 6), (6, 6), (12, 6), (18, 6))
 A_HALF = tuple(lo // 14 for lo, _ in A_PIECES)
 ORDER = (
-    (0, 2, 0), (0, 4, 0), (0, 12, 0), (1, 2, 0), (1, 6, 0), (0, 1, 0), (0, 1, 1), (0, 1, 2), (0, 1, 3), (0, 1, 4),
-    (0, 1, 5), (0, 4, 1), (0, 12, 1), (1, 1, 0), (1, 2, 2), (1, 6, 2), (0, 13, 0), (0, 5, 0), (0, 3, 0), (0, 4, 2),
-    (0, 12, 2), (0, 2, 1), (0, 4, 3), (0, 13, 1), (0, 8, 0), (1, 4, 0), (0, 5, 1), (1, 3, 0), (0, 12, 3), (1, 1, 2),
-    (0, 8, 2), (0, 13, 2), (0, 5, 2), (0, 3, 1), (1, 7, 0), (1, 2, 1), (0, 5, 3), (0, 2, 2), (0, 8, 1), (0, 9, 0),
-    (0, 6, 1), (0, 13, 3), (0, 14, 0), (1, 6, 1), (1, 2, 3), (0, 9, 2), (0, 14, 1), (0, 4, 4), (0, 2, 3), (0, 9, 1),
-    (0, 8, 3), (0, 3, 2), (0, 7, 1), (0, 12, 4), (1, 6, 3), (1, 4, 2), (0, 6, 0), (0, 15, 0), (0, 15, 1), (0, 6, 2),
-    (0, 5, 4), (0, 14, 2), (0, 3, 3), (1, 7, 2), (1, 3, 2), (1, 1, 1), (0, 9, 3), (0, 13, 4), (0, 7, 0), (0, 4, 5),
-    (0, 12, 5), (1, 5, 0), (1, 4, 3), (0, 7, 2), (1, 1, 3), (0, 15, 2), (0, 10, 2), (0, 10, 1), (0, 2, 4), (1, 4, 1),
-    (1, 5, 2), (0, 5, 5), (0, 13, 5), (0, 8, 4), (0, 8, 5), (0, 2, 5), (1, 7, 1), (0, 11, 2), (1, 3, 1), (0, 11, 1),
-    (0, 6, 4), (0, 14, 4), (0, 6, 3), (0, 3, 4), (1, 7, 3), (0, 9, 4), (0, 9, 5), (1, 3, 3), (0, 10, 0), (0, 6, 5),
-    (0, 14, 5), (0, 3, 5), (0, 14, 3), (0, 15, 4), (0, 7, 4), (0, 7, 3), (1, 5, 1), (0, 10, 3), (0, 10, 4), (1, 5, 3),
-    (0, 11, 0), (0, 10, 5), (0, 15, 5), (0, 7, 5), (0, 15, 3), (0, 11, 3), (0, 11, 4), (0, 11, 5),
+    (0, 1, 6), (1, 2, 3), (1, 1, 1), (1, 2, 2), (1, 1, 0), (0, 12, 5), (0, 1, 7), (0, 4, 1), (0, 4, 5), (1, 7, 1),
+    (0, 12, 2), (0, 4, 3), (0, 12, 1), (1, 3, 1), (1, 6, 1), (0, 12, 3), (1, 4, 2), (0, 12, 4), (0, 4, 2), (0, 12, 0),
+    (1, 6, 0), (0, 4, 0), (1, 1, 2), (0, 13, 7), (0, 8, 1), (1, 3, 0), (0, 2, 3), (0, 8, 5), (1, 4, 1), (0, 2, 5),
+    (0, 4, 4), (1, 4, 3), (0, 8, 4), (0, 13, 6), (0, 8, 3), (0, 2, 0), (0, 8, 0), (0, 2, 4), (1, 2, 0), (0, 8, 2),
+    (0, 2, 1), (0, 2, 2), (1, 7, 0), (0, 9, 7), (0, 5, 7), (1, 5, 1), (1, 3, 2), (0, 9, 6), (0, 3, 7), (0, 3, 6),
+    (0, 14, 5), (1, 6, 2), (1, 1, 3), (1, 7, 2), (0, 6, 5), (0, 6, 4), (0, 14, 4), (0, 5, 6), (1, 4, 0), (0, 6, 3),
+    (0, 14, 1), (0, 14, 3), (1, 2, 1), (1, 5, 0), (0, 7, 7), (0, 15, 7), (0, 6, 2), (0, 6, 1), (0, 14, 0), (0, 14, 2),
+    (1, 5, 2), (0, 6, 0), (1, 7, 3), (1, 3, 3), (0, 15, 6), (0, 10, 5), (0, 10, 3), (0, 10, 4), (0, 7, 6), (1, 6, 3),
+    (0, 10, 0), (0, 10, 1), (0, 10, 2), (0, 11, 7), (1, 5, 3), (0, 11, 6),
 )
 COPIES = (
-    (0, 0, 0, 12, 0, 0), (0, 0, 0, 4, 0, 1), (0, 0, 0, 2, 0, 2), (0, 0, 0, 1, 0, 6), (0, 1, 0, 6, 0, 3), (0, 1, 0, 2, 0, 4),
-    (0, 1, 0, 1, 0, 5), (0, 0, 0, 12, 1, 0), (0, 0, 0, 4, 1, 1), (0, 0, 0, 2, 1, 2), (0, 0, 0, 1, 1, 6), (0, 1, 0, 6, 2, 3),
-    (0, 1, 0, 2, 2, 4), (0, 1, 0, 1, 2, 5), (0, 0, 0, 12, 2, 0), (0, 0, 0, 4, 2, 1), (0, 0, 0, 2, 2, 2), (0, 0, 0, 1, 2, 6),
-    (0, 0, 0, 1, 3, 6), (0, 0, 0, 1, 4, 6), (0, 0, 0, 1, 5, 6), (1, 0, 2, 3, 0, 6), (1, 0, 0, 12, 3, 0), (1, 0, 0, 4, 3, 1),
-    (2, 0, 4, 6, 0, 2), (2, 0, 4, 5, 0, 6), (3, 0, 12, 8, 0, 0), (3, 0, 12, 14, 0, 2), (3, 0, 12, 13, 0, 6), (3, 0, 0, 2, 3, 2),
-    (5, 1, 6, 4, 0, 3), (5, 1, 0, 1, 1, 5), (5, 1, 0, 1, 3, 5), (12, 0, 4, 5, 1, 6), (13, 0, 12, 8, 1, 0), (13, 0, 12, 13, 1, 6),
-    (13, 0, 0, 2, 4, 2), (14, 1, 1, 7, 0, 3), (14, 1, 1, 3, 0, 4), (14, 1, 0, 6, 1, 3), (14, 1, 0, 2, 1, 4), (14, 1, 0, 6, 3, 3),
-    (14, 1, 0, 2, 3, 4), (15, 1, 2, 4, 2, 4), (20, 0, 4, 8, 2, 1), (20, 0, 4, 5, 2, 6), (21, 0, 12, 13, 2, 6), (21, 0, 0, 2, 5, 2),
-    (22, 0, 2, 14, 1, 0), (22, 0, 2, 6, 1, 1), (22, 0, 2, 3, 1, 6), (22, 0, 0, 12, 4, 0), (22, 0, 0, 4, 4, 1), (23, 0, 4, 8, 3, 1),
-    (23, 0, 4, 6, 3, 2), (23, 0, 4, 5, 3, 6), (25, 0, 8, 10, 0, 2), (25, 0, 8, 9, 0, 6), (29, 0, 12, 14, 3, 2), (29, 0, 12, 13, 3, 6),
-    (30, 1, 1, 7, 2, 3), (30, 1, 1, 3, 2, 4), (31, 0, 8, 9, 2, 6), (35, 1, 7, 5, 0, 3), (38, 0, 2, 14, 2, 0), (38, 0, 2, 6, 2, 1),
-    (38, 0, 2, 3, 2, 6), (38, 0, 0, 12, 5, 0), (38, 0, 0, 4, 5, 1), (39, 0, 8, 9, 1, 6), (41, 0, 6, 7, 1, 6), (43, 0, 14, 15, 0, 6),
-    (44, 1, 6, 4, 1, 3), (45, 1, 2, 4, 3, 4), (47, 0, 14, 10, 1, 0), (47, 0, 14, 15, 1, 6), (48, 0, 4, 5, 4, 6), (49, 0, 2, 3, 3, 6),
-    (51, 0, 8, 10, 3, 2), (51, 0, 8, 9, 3, 6), (54, 0, 12, 8, 4, 0), (54, 0, 12, 13, 4, 6), (57, 0, 6, 7, 0, 6), (60, 0, 6, 10, 2, 1),
-    (60, 0, 6, 7, 2, 6), (62, 0, 14, 15, 2, 6), (65, 1, 3, 5, 2, 4), (66, 1, 1, 7, 1, 3), (66, 1, 1, 3, 1, 4), (70, 0, 4, 8, 5, 1),
-    (70, 0, 4, 5, 5, 6), (71, 0, 12, 13, 5, 6), (75, 1, 1, 7, 3, 3), (75, 1, 1, 3, 3, 4), (77, 0, 10, 11, 2, 6), (78, 0, 10, 11, 1, 6),
-    (79, 0, 2, 14, 4, 0), (79, 0, 2, 6, 4, 1), (79, 0, 2, 3, 4, 6), (84, 0, 8, 9, 4, 6), (85, 0, 8, 9, 5, 6), (86, 0, 2, 14, 5, 0),
-    (86, 0, 2, 6, 5, 1), (86, 0, 2, 3, 5, 6), (87, 1, 7, 5, 1, 3), (91, 0, 6, 7, 4, 6), (92, 0, 14, 10, 4, 0), (92, 0, 14, 15, 4, 6),
-    (93, 0, 6, 7, 3, 6), (98, 1, 3, 5, 3, 4), (99, 0, 10, 11, 0, 6), (100, 0, 6, 10, 5, 1), (100, 0, 6, 7, 5, 6), (101, 0, 14, 15, 5, 6),
-    (103, 0, 14, 15, 3, 6), (108, 0, 10, 11, 3, 6), (109, 0, 10, 11, 4, 6), (112, 0, 10, 11, 5, 6),
+    (0, 0, 0, 4, 1, 1), (0, 1, 0, 1, 1, 5), (0, 1, 0, 6, 0, 3), (0, 0, 0, 1, 6, 6), (0, 0, 0, 4, 3, 1), (0, 1, 0, 2, 3, 4),
+    (0, 0, 0, 12, 5, 0), (0, 1, 0, 6, 1, 3), (0, 0, 0, 4, 5, 1), (1, 0, 0, 4, 4, 1), (1, 0, 0, 4, 2, 1), (1, 0, 0, 12, 1, 0),
+    (1, 0, 0, 1, 7, 6), (1, 1, 0, 1, 0, 5), (1, 0, 0, 4, 0, 1), (1, 1, 0, 2, 2, 4), (2, 1, 0, 1, 2, 5), (2, 0, 0, 12, 0, 0),
+    (2, 1, 2, 4, 3, 4), (3, 1, 1, 7, 1, 3), (3, 0, 0, 12, 4, 0), (3, 0, 0, 2, 2, 2), (3, 0, 0, 2, 4, 2), (3, 1, 1, 3, 1, 4),
+    (4, 1, 2, 4, 2, 4), (5, 1, 1, 7, 0, 3), (5, 1, 1, 3, 0, 4), (8, 0, 0, 12, 2, 0), (8, 0, 0, 2, 3, 2), (9, 0, 0, 2, 5, 2),
+    (9, 0, 0, 12, 3, 0), (9, 0, 4, 8, 5, 1), (10, 1, 7, 5, 1, 3), (10, 0, 0, 2, 0, 2), (11, 0, 0, 2, 1, 2), (12, 0, 4, 8, 3, 1),
+    (12, 1, 0, 1, 3, 5), (12, 0, 4, 6, 3, 2), (13, 0, 12, 8, 1, 0), (15, 1, 6, 4, 1, 3), (15, 1, 0, 2, 0, 4), (16, 0, 12, 14, 3, 2),
+    (18, 0, 12, 8, 4, 0), (18, 0, 12, 13, 7, 6), (19, 0, 4, 8, 2, 1), (20, 0, 12, 14, 0, 2), (20, 0, 12, 8, 0, 0), (20, 0, 12, 13, 6, 6),
+    (21, 1, 6, 4, 0, 3), (22, 1, 0, 6, 2, 3), (22, 0, 4, 6, 0, 2), (22, 0, 4, 5, 6, 6), (23, 1, 1, 3, 2, 4), (23, 1, 1, 7, 2, 3),
+    (30, 0, 2, 6, 5, 1), (30, 0, 2, 14, 5, 0), (31, 0, 4, 5, 7, 6), (35, 0, 8, 10, 3, 2), (35, 0, 8, 9, 7, 6), (37, 0, 8, 10, 0, 2),
+    (38, 0, 2, 14, 4, 0), (38, 1, 0, 2, 1, 4), (38, 0, 2, 6, 4, 1), (38, 0, 2, 3, 7, 6), (40, 0, 8, 9, 6, 6), (41, 0, 2, 6, 1, 1),
+    (41, 0, 2, 14, 1, 0), (42, 0, 2, 14, 2, 0), (42, 0, 2, 6, 2, 1), (42, 0, 2, 3, 6, 6), (43, 1, 7, 5, 0, 3), (47, 1, 3, 5, 2, 4),
+    (53, 1, 1, 7, 3, 3), (53, 1, 1, 3, 3, 4), (55, 0, 6, 10, 5, 1), (57, 0, 14, 10, 4, 0), (60, 1, 0, 6, 3, 3), (60, 0, 6, 7, 7, 6),
+    (61, 0, 14, 10, 1, 0), (62, 0, 14, 15, 7, 6), (67, 0, 6, 10, 2, 1), (70, 0, 14, 15, 6, 6), (72, 0, 6, 7, 6, 6), (74, 1, 3, 5, 3, 4),
+    (78, 0, 10, 11, 7, 6), (83, 0, 10, 11, 6, 6),
 )
 TARGETS = ("y+", "y-", "zl", "x+", "x-", "zh", "sib")
 
@@ -70,10 +62,13 @@
 
 
 NOTHING = 127
+OWN = 10
 WHEN_A, WHEN_B, TRIGGERS = make_plan()
-
-
-def kernel(a_hbm, b_hbm, a_rows, b_cols, screen, keep, owners, out, a_in, b_in, a_all, b_all, total, dense, stage, lists, meta_a,
+LENGTHS = [(B_PIECES if copy[1] else A_PIECES)[copy[4]][1] for copy in COPIES]
+SENT = [sorted(range(len(COPIES)), key=lambda i: (LENGTHS[i], i)).index(n) for n in range(len(COPIES))]
+
+
+def kernel(a_hbm, b_hbm, rows_hbm, cols_hbm, screen_hbm, keep_hbm, owners_hbm, out, a_rows, b_cols, screen, keep, owners, a_in, b_in, a_all, b_all, total, dense, stage, lists, meta_a,
            meta_b, owned_m, owned_f, a_recv, b_recv, sent, ma_send, ma_recv, mb_send, mb_recv, out_send, out_recv, own_sem, in_sem):
     row, col = lax.axis_index("row"), lax.axis_index("col")
     rem, div = lax.rem, lax.div
@@ -89,11 +84,6 @@
         "zh": (row + 1 - 2 * zh, col),
     }
 
-    load_a = pltpu.make_async_copy(a_hbm, a_in, in_sem.at[0])
-    load_b = pltpu.make_async_copy(b_hbm, b_in, in_sem.at[1])
-    load_a.start()
-    load_b.start()
-
     barrier = pltpu.get_barrier_semaphore()
 
     @pl.loop(1, 16)
@@ -103,6 +93,15 @@
     @pl.loop(1, 8)
     def _(t):
         pl.semaphore_signal(barrier, inc=1, device_id=(rem(row + t, 8), col), device_id_type=MESH)
+
+    loads = [
+        pltpu.make_async_copy(source, there, in_sem.at[i]) for i, (source, there) in enumerate((
+            (rows_hbm, a_rows), (cols_hbm, b_cols), (a_hbm, a_in), (b_hbm, b_in), (screen_hbm, screen), (keep_hbm, keep),
+            (owners_hbm, owners)))]
+    for load in loads:
+        load.start()
+    loads[0].wait()
+    loads[1].wait()
 
     def note(at, value):
         lists[at] = value
@@ -133,16 +132,20 @@
                 note(64 + h * 16 + k * 4 + c, places[c])
             note(96 + h * 4 + k, gone)
 
-    load_a.wait()
-    for k in range(4):
-        gone = lists[32 + k]
-        for n in range(7):
-            a_all[0, k * 7 + n] = a_in[k, lists[k * 8 + n + jnp.where(n >= gone, 1, 0)]]
-    load_b.wait()
-    for hk in range(8):
-        gone = lists[96 + hk]
-        for n in range(3):
-            b_all[0, hk * 3 + n] = b_in[hk, lists[64 + hk * 4 + n + jnp.where(n >= gone, 1, 0)]]
+    def sort_half(half):
+        for k in range(2 * half, 2 * half + 2):
+            gone = lists[32 + k]
+            for n in range(7):
+                a_all[0, k * 7 + n] = a_in[k, lists[k * 8 + n + jnp.where(n >= gone, 1, 0)]]
+        if half == 0:
+            loads[3].wait()
+        for hk in (2 * half, 2 * half + 1, 2 * half + 4, 2 * half + 5):
+            gone = lists[96 + hk]
+            for n in range(3):
+                b_all[0, hk * 3 + n] = b_in[hk, lists[64 + hk * 4 + n + jnp.where(n >= gone, 1, 0)]]
+
+    loads[2].wait()
+    sort_half(0)
 
     def copy_of(number):
         _, kind, slot, there, piece, target = COPIES[number]
@@ -150,7 +153,7 @@
         lo, n = pieces[piece]
         return pltpu.make_async_remote_copy(
             src_ref=ref.at[slot, pl.ds(lo, n)], dst_ref=ref.at[there, pl.ds(lo, n)],
-            send_sem=sent.at[number], recv_sem=recv.at[there * len(pieces) + piece],
+            send_sem=sent.at[SENT[number]], recv_sem=recv.at[there * len(pieces) + piece],
             device_id=targets[TARGETS[target]], device_id_type=MESH)
 
     def arrival_of(kind, slot, piece):
@@ -171,8 +174,12 @@
             src_ref=lists, dst_ref=meta_b.at[row], send_sem=mb_send.at[t], recv_sem=mb_recv.at[row],
             device_id=(rem(row + t, 8), col), device_id_type=MESH)
 
+    def in_half(copy):
+        return B_PIECES[copy[4]][0] // 6 % 2 if copy[1] else A_HALF[copy[4]]
+
     pl.semaphore_wait(barrier, 22)
-
+    own = [(number, copy) for number, copy in enumerate(COPIES) if copy[0] == 0]
+    first = [number for number, copy in own if in_half(copy) == 0]
     @pl.loop(1, 16)
     def _(t):
         meta_a_copy(t).start()
@@ -181,9 +188,15 @@
     def _(t):
         meta_b_copy(t).start()
 
-    for number, copy in enumerate(COPIES):
-        if copy[0] == 0:
+    for number in first:
+        copy_of(number).start()
+    sort_half(1)
+    for number, copy in own:
+        if in_half(copy) == 1:
             copy_of(number).start()
+
+    for load in loads[4:]:
+        load.wait()
 
     @pl.loop(0, 16)
     def _(o):
@@ -250,10 +263,10 @@
             total[c * 8:(c + 1) * 8] += part.reshape(8, W, W)
 
     def pair_of(s):
-        g, e = rem(col + s, 16), rem(row + s, 16)
-        p, h = rem(e, 8), div(e, 8)
-        qa = 4 * rem(div(g, 4) - y + 4, 4) + 2 * rem(rem(div(g, 2), 2) + zl, 2) + rem(rem(g, 2) + core, 2)
-        qb = 2 * rem(div(p, 2) - x + 4, 4) + rem(rem(p, 2) + zh, 2)
+        g, e = (col + s) & 15, (row + s) & 15
+        p, h = e & 7, e >> 3
+        qa = 4 * (((g >> 2) - y) & 3) + 2 * (((g >> 1) & 1) ^ zl) + ((g & 1) ^ core)
+        qb = 2 * (((p >> 1) - x) & 3) + ((p & 1) ^ zh)
         return g, p, h, qa, qb
 
     def ready_after(n):
@@ -262,19 +275,19 @@
             return I32(-1)
         half, which = code % 2, code // 2 % 16
         if code < 32:
-            g = 4 * rem(y + which // 4, 4) + 2 * rem(zl + which // 2 % 2, 2) + rem(core + which % 2, 2)
-            s = rem(g - col + 16, 16)
+            g = 4 * ((y + which // 4) & 3) + 2 * (zl ^ (which // 2 % 2)) + (core ^ (which % 2))
+            s = (g - col) & 15
             _, _, h, _, qb = pair_of(s)
             there = [WHEN_B[at * 2 + half] <= n for at in range(16)]
             at = 2 * qb + h
         else:
-            p = 2 * rem(x + which // 4, 4) + rem(zh + which // 2 % 2, 2)
-            s = rem(p + 8 * (which % 2) - row + 16, 16)
+            p = 2 * ((x + which // 4) & 3) + (zh ^ (which // 2 % 2))
+            s = (p + 8 * (which % 2) - row) & 15
             at = pair_of(s)[3]
             there = [WHEN_A[at * 2 + half] < n for at in range(16)]
         if not any(there):
             return I32(-1)
-        both = rem(lax.shift_right_logical(I32(sum(1 << i for i, v in enumerate(there) if v)), at), 2)
+        both = lax.shift_right_logical(I32(sum(1 << i for i, v in enumerate(there) if v)), at) & 1
         return jnp.where(both == 1, 2 * s + half, -1)
 
     def receive(n, low, high):
@@ -293,62 +306,81 @@
 
         @pl.when(code >= 0)
         def _():
-            s, half = div(code, 2), rem(code, 2)
+            s, half = code >> 1, code & 1
             g, p, h, qa, qb = pair_of(s)
             multiply(qa, half, qb, h, s, g, p)
 
-    def out_copy(t):
-        o = rem(col + t, 16)
+    def owner_at(u):
+        dy, dz, dk = rem(2 + 3 * u, 4), 1 - div(u, 8), rem(div(u, 4), 2)
+        return 4 * rem(y + dy, 4) + 2 * rem(zl + dz, 2) + rem(core + dk, 2)
+
+    def out_copy(u):
         return pltpu.make_async_remote_copy(
-            src_ref=stage.at[t], dst_ref=out.at[col], send_sem=out_send.at[t], recv_sem=out_recv.at[col],
-            device_id=(row, o), device_id_type=MESH)
+            src_ref=stage.at[u], dst_ref=out.at[col], send_sem=out_send.at[u], recv_sem=out_recv.at[col],
+            device_id=(row, owner_at(u)), device_id_type=MESH)
+
+    def own_copy():
+        return pltpu.make_async_copy(stage.at[OWN], out.at[col], own_sem)
 
     @pl.loop(0, 16)
     def _(u):
-        t = rem(u + 8, 16)
-        o = rem(col + t, 16)
+        o = owner_at(u)
         for slot in range(2):
-            stage[t, slot] = (total[owned_m[2 * o + slot]] * owned_f[2 * o + slot]).astype(BF16)
-
-        @pl.when(t != 0)
+            stage[u, slot] = (total[owned_m[2 * o + slot]] * owned_f[2 * o + slot]).astype(BF16)
+
+        @pl.when(u != OWN)
         def _():
-            out_copy(t).start()
-
-        @pl.when(t == 0)
+            out_copy(u).start()
+
+        @pl.when(u == OWN)
         def _():
-            pltpu.make_async_copy(stage.at[0], out.at[col], own_sem).start()
-
-    pltpu.make_async_copy(stage.at[0], out.at[col], own_sem).wait()
+            own_copy().start()
 
     @pl.loop(1, 16)
     def _(t):
         meta_a_copy(t).wait_send()
-        out_copy(t).wait_send()
 
     @pl.loop(1, 8)
     def _(t):
         meta_b_copy(t).wait_send()
 
-    for number in range(len(COPIES)):
-        copy_of(number).wait_send()
-
-    @pl.loop(1, 16)
-    def _(t):
-        source = rem(col + t, 16)
-        pltpu.make_async_remote_copy(
-            src_ref=stage.at[t], dst_ref=out.at[source], send_sem=out_send.at[t], recv_sem=out_recv.at[source],
-            device_id=(row, source), device_id_type=MESH).wait_recv()
+    for length in sorted(set(LENGTHS)):
+        some = [SENT[number] for number, its in enumerate(LENGTHS) if its == length]
+
+        @pl.loop(min(some), max(some) + 1)
+        def _(at, length=length):
+            block = a_all.at[0, pl.ds(0, length)]
+            pltpu.make_async_remote_copy(
+                src_ref=block, dst_ref=block, send_sem=sent.at[at], recv_sem=a_recv.at[0],
+                device_id=targets["sib"], device_id_type=MESH).wait_send()
+
+    @pl.loop(0, 16)
+    def _(u):
+        @pl.when(u != OWN)
+        def _():
+            out_copy(u).wait_send()
+            source = owner_at(u)
+            pltpu.make_async_remote_copy(
+                src_ref=stage.at[u], dst_ref=out.at[source], send_sem=out_send.at[u], recv_sem=out_recv.at[source],
+                device_id=(row, source), device_id_type=MESH).wait_recv()
+
+    own_copy().wait()
 
 
 def on_device(a_blocks, a_rows, b_blocks, b_cols, screen, keep, owners):
-    hbm, smem = pl.BlockSpec(memory_space=pl.ANY), pl.BlockSpec(memory_space=pltpu.SMEM)
+    hbm = pl.BlockSpec(memory_space=pl.ANY)
     dma = pltpu.SemaphoreType.DMA
     out = pl.pallas_call(
         kernel,
         out_shape=jax.ShapeDtypeStruct((16, 2, W, W), BF16),
-        in_specs=[hbm, hbm, smem, smem, smem, smem, smem],
+        in_specs=[hbm] * 7,
         out_specs=hbm,
         scratch_shapes=[
+            pltpu.SMEM((4, 7), I32),
+            pltpu.SMEM((3, 2, 4), I32),
+            pltpu.SMEM((7, 3, 4, 16), I32),
+            pltpu.SMEM((32,), I32),
+            pltpu.SMEM((32,), I32),
             pltpu.VMEM((4, 7, W, W), BF16),
             pltpu.VMEM((8, 3, W, W), BF16),
             pltpu.VMEM((16, 28, W, W), BF16),
@@ -371,7 +403,7 @@
             dma((16,)),
             dma((16,)),
             dma,
-            dma((2,)),
+            dma((7,)),
         ],
         compiler_params=pltpu.CompilerParams(
             collective_id=0, has_side_effects=True, vmem_limit_bytes=60 * 2**20),

time: 90.2 us -> 87.1 us (0.966)
  Pallas kernels: 87.6 us -> 84.6 us
    pallas_call x1, Pallas kernels: 87.6 us -> 84.6 us  [on_device(): pl.pallas_call(kernel, out_shape=jax.ShapeDtypeStruct((16, 2, W, W), BF16...]
where the time goes in v4:
time: 87.1 us; the launch traced here: 86.9 us
  Pallas kernels  84.6 us (97%)
  local copies, waits for them, and re-layouts  2.31 us (3%)
    pallas_call x1, Pallas kernels, on_device(): pl.pallas_call(kernel, out_shape=jax.ShapeDtypeStruct((16, 2, W, W), BF16...  84.6 us
    unnamed x1, local copies, waits for them, and re-layouts  2.31 us

profile of v4, /device:TPU:1, one launch (start us, length us, event | category | flops | bytes accessed | tf_op | source)
XLA Modules:
  0.0 86.9 jit_solution(16572299916543648335)
XLA Ops:
  0.0 84.6 %gather_multiply_send.1 = bf16[16,2,128,128]{3,2,1,0:T(8,128)(2,1)} custom-call(bf16[4,7,128,128]{3,2,1,0:T(8,128)(2,1)} %bitcast.13, bf16[8,3,128,128]{3,2,1,0:T(8,128)(2,1)} %bitcast.14, s32[4,7]{1,0:T(4,128)} %bitcast.17, s32[3,2,4]{2,1,0:T(2,128)} %bitcast.16, s32[7,3,4,16]{3,2,1,0:T(4,128)} %bitcast.15, s32[32]{0:T(128)} %bitcast.18, s32[32]{0:T(128)} %bitcast.19), custom_call_target="tpu_custom_call" | custom-call | flops 8600000512 | bytes 4000000 | tf_op jit(solution)/shard_map/gather_multiply_send/pallas_call | solution.py:373
  84.6 2.3 %copy.9 = bf16[1,1,16,2,128,128]{5,4,3,2,1,0:T(8,128)(2,1)} copy(bf16[1,1,16,2,128,128]{5,4,3,2,1,0:T(8,128)(2,1)} %bitcast.12) | data formatting | bytes 2097152

commit v5 on v4

--- a/solution.py
+++ b/solution.py
@@ -11,36 +11,36 @@
 BF16, F32, I32 = jnp.bfloat16, jnp.float32, jnp.int32
 W = 128
 
-A_PIECES = ((0, 4), (4, 5), (9, 5), (14, 3), (17, 5), (22, 6), (0, 14), (14, 14))
+A_PIECES = ((0, 3), (3, 5), (8, 6), (14, 3), (17, 5), (22, 6), (0, 14), (14, 14))
 B_PIECES = ((0, 6), (6, 6), (12, 6), (18, 6))
 A_HALF = tuple(lo // 14 for lo, _ in A_PIECES)
 ORDER = (
-    (0, 1, 6), (1, 2, 3), (1, 1, 1), (1, 2, 2), (1, 1, 0), (0, 12, 5), (0, 1, 7), (0, 4, 1), (0, 4, 5), (1, 7, 1),
-    (0, 12, 2), (0, 4, 3), (0, 12, 1), (1, 3, 1), (1, 6, 1), (0, 12, 3), (1, 4, 2), (0, 12, 4), (0, 4, 2), (0, 12, 0),
-    (1, 6, 0), (0, 4, 0), (1, 1, 2), (0, 13, 7), (0, 8, 1), (1, 3, 0), (0, 2, 3), (0, 8, 5), (1, 4, 1), (0, 2, 5),
-    (0, 4, 4), (1, 4, 3), (0, 8, 4), (0, 13, 6), (0, 8, 3), (0, 2, 0), (0, 8, 0), (0, 2, 4), (1, 2, 0), (0, 8, 2),
-    (0, 2, 1), (0, 2, 2), (1, 7, 0), (0, 9, 7), (0, 5, 7), (1, 5, 1), (1, 3, 2), (0, 9, 6), (0, 3, 7), (0, 3, 6),
-    (0, 14, 5), (1, 6, 2), (1, 1, 3), (1, 7, 2), (0, 6, 5), (0, 6, 4), (0, 14, 4), (0, 5, 6), (1, 4, 0), (0, 6, 3),
-    (0, 14, 1), (0, 14, 3), (1, 2, 1), (1, 5, 0), (0, 7, 7), (0, 15, 7), (0, 6, 2), (0, 6, 1), (0, 14, 0), (0, 14, 2),
-    (1, 5, 2), (0, 6, 0), (1, 7, 3), (1, 3, 3), (0, 15, 6), (0, 10, 5), (0, 10, 3), (0, 10, 4), (0, 7, 6), (1, 6, 3),
-    (0, 10, 0), (0, 10, 1), (0, 10, 2), (0, 11, 7), (1, 5, 3), (0, 11, 6),
+    (0, 4, 0), (1, 1, 2), (1, 2, 3), (0, 12, 1), (1, 2, 2), (1, 6, 1), (0, 4, 1), (1, 1, 0), (1, 2, 0), (0, 12, 4),
+    (0, 4, 2), (1, 4, 1), (1, 7, 2), (0, 6, 0), (0, 1, 7), (1, 1, 1), (1, 3, 2), (0, 12, 0), (0, 5, 6), (0, 2, 0),
+    (0, 4, 3), (1, 6, 0), (1, 7, 0), (0, 4, 5), (0, 8, 1), (0, 2, 2), (0, 12, 2), (0, 1, 6), (1, 4, 3), (0, 12, 3),
+    (0, 2, 1), (0, 8, 0), (1, 7, 1), (0, 8, 2), (0, 12, 5), (1, 4, 2), (0, 3, 6), (0, 4, 4), (1, 3, 0), (0, 9, 6),
+    (1, 4, 0), (0, 13, 6), (0, 2, 5), (0, 14, 1), (0, 5, 7), (0, 6, 1), (0, 14, 2), (0, 2, 4), (0, 13, 7), (0, 6, 2),
+    (1, 5, 0), (0, 8, 4), (1, 1, 3), (0, 8, 5), (0, 8, 3), (1, 5, 2), (0, 7, 6), (0, 2, 3), (0, 14, 0), (1, 3, 1),
+    (1, 6, 2), (1, 2, 1), (0, 14, 5), (0, 6, 5), (0, 3, 7), (1, 5, 1), (0, 9, 7), (0, 14, 3), (0, 15, 6), (0, 6, 3),
+    (0, 6, 4), (1, 3, 3), (1, 6, 3), (0, 10, 0), (0, 14, 4), (0, 10, 2), (0, 7, 7), (0, 10, 1), (1, 7, 3), (0, 15, 7),
+    (0, 10, 3), (0, 10, 5), (0, 10, 4), (0, 11, 6), (1, 5, 3), (0, 11, 7),
 )
 COPIES = (
-    (0, 0, 0, 4, 1, 1), (0, 1, 0, 1, 1, 5), (0, 1, 0, 6, 0, 3), (0, 0, 0, 1, 6, 6), (0, 0, 0, 4, 3, 1), (0, 1, 0, 2, 3, 4),
-    (0, 0, 0, 12, 5, 0), (0, 1, 0, 6, 1, 3), (0, 0, 0, 4, 5, 1), (1, 0, 0, 4, 4, 1), (1, 0, 0, 4, 2, 1), (1, 0, 0, 12, 1, 0),
-    (1, 0, 0, 1, 7, 6), (1, 1, 0, 1, 0, 5), (1, 0, 0, 4, 0, 1), (1, 1, 0, 2, 2, 4), (2, 1, 0, 1, 2, 5), (2, 0, 0, 12, 0, 0),
-    (2, 1, 2, 4, 3, 4), (3, 1, 1, 7, 1, 3), (3, 0, 0, 12, 4, 0), (3, 0, 0, 2, 2, 2), (3, 0, 0, 2, 4, 2), (3, 1, 1, 3, 1, 4),
-    (4, 1, 2, 4, 2, 4), (5, 1, 1, 7, 0, 3), (5, 1, 1, 3, 0, 4), (8, 0, 0, 12, 2, 0), (8, 0, 0, 2, 3, 2), (9, 0, 0, 2, 5, 2),
-    (9, 0, 0, 12, 3, 0), (9, 0, 4, 8, 5, 1), (10, 1, 7, 5, 1, 3), (10, 0, 0, 2, 0, 2), (11, 0, 0, 2, 1, 2), (12, 0, 4, 8, 3, 1),
-    (12, 1, 0, 1, 3, 5), (12, 0, 4, 6, 3, 2), (13, 0, 12, 8, 1, 0), (15, 1, 6, 4, 1, 3), (15, 1, 0, 2, 0, 4), (16, 0, 12, 14, 3, 2),
-    (18, 0, 12, 8, 4, 0), (18, 0, 12, 13, 7, 6), (19, 0, 4, 8, 2, 1), (20, 0, 12, 14, 0, 2), (20, 0, 12, 8, 0, 0), (20, 0, 12, 13, 6, 6),
-    (21, 1, 6, 4, 0, 3), (22, 1, 0, 6, 2, 3), (22, 0, 4, 6, 0, 2), (22, 0, 4, 5, 6, 6), (23, 1, 1, 3, 2, 4), (23, 1, 1, 7, 2, 3),
-    (30, 0, 2, 6, 5, 1), (30, 0, 2, 14, 5, 0), (31, 0, 4, 5, 7, 6), (35, 0, 8, 10, 3, 2), (35, 0, 8, 9, 7, 6), (37, 0, 8, 10, 0, 2),
-    (38, 0, 2, 14, 4, 0), (38, 1, 0, 2, 1, 4), (38, 0, 2, 6, 4, 1), (38, 0, 2, 3, 7, 6), (40, 0, 8, 9, 6, 6), (41, 0, 2, 6, 1, 1),
-    (41, 0, 2, 14, 1, 0), (42, 0, 2, 14, 2, 0), (42, 0, 2, 6, 2, 1), (42, 0, 2, 3, 6, 6), (43, 1, 7, 5, 0, 3), (47, 1, 3, 5, 2, 4),
-    (53, 1, 1, 7, 3, 3), (53, 1, 1, 3, 3, 4), (55, 0, 6, 10, 5, 1), (57, 0, 14, 10, 4, 0), (60, 1, 0, 6, 3, 3), (60, 0, 6, 7, 7, 6),
-    (61, 0, 14, 10, 1, 0), (62, 0, 14, 15, 7, 6), (67, 0, 6, 10, 2, 1), (70, 0, 14, 15, 6, 6), (72, 0, 6, 7, 6, 6), (74, 1, 3, 5, 3, 4),
-    (78, 0, 10, 11, 7, 6), (83, 0, 10, 11, 6, 6),
+    (0, 0, 0, 12, 1, 0), (0, 0, 0, 4, 0, 1), (0, 1, 0, 1, 2, 5), (0, 1, 0, 2, 2, 4), (0, 0, 0, 12, 0, 0), (0, 1, 0, 6, 1, 3),
+    (0, 1, 0, 2, 3, 4), (0, 0, 0, 4, 2, 1), (0, 0, 0, 12, 5, 0), (0, 0, 0, 1, 7, 6), (0, 0, 0, 4, 1, 1), (0, 0, 0, 4, 4, 1),
+    (0, 0, 0, 2, 0, 2), (0, 1, 0, 1, 0, 5), (1, 1, 0, 6, 0, 3), (1, 1, 0, 1, 1, 5), (1, 0, 0, 4, 5, 1), (1, 0, 4, 6, 0, 2),
+    (1, 1, 0, 2, 0, 4), (2, 1, 1, 7, 2, 3), (2, 1, 1, 3, 2, 4), (2, 0, 0, 12, 4, 0), (3, 0, 0, 1, 6, 6), (3, 0, 0, 12, 2, 0),
+    (3, 1, 2, 4, 3, 4), (4, 0, 12, 8, 1, 0), (4, 0, 0, 2, 2, 2), (4, 0, 0, 4, 3, 1), (5, 1, 2, 4, 2, 4), (6, 0, 0, 12, 3, 0),
+    (6, 1, 6, 4, 1, 3), (8, 1, 1, 3, 0, 4), (8, 1, 1, 7, 0, 3), (9, 0, 0, 2, 1, 2), (11, 0, 0, 2, 5, 2), (11, 0, 4, 8, 2, 1),
+    (11, 0, 4, 5, 6, 6), (12, 0, 0, 2, 4, 2), (14, 1, 0, 1, 3, 5), (16, 1, 1, 3, 1, 4), (16, 1, 1, 7, 1, 3), (17, 1, 3, 5, 2, 4),
+    (17, 0, 0, 2, 3, 2), (18, 0, 12, 14, 0, 2), (18, 0, 12, 8, 0, 0), (21, 0, 4, 6, 3, 2), (21, 0, 4, 8, 3, 1), (22, 1, 6, 4, 0, 3),
+    (23, 1, 7, 5, 0, 3), (26, 0, 2, 6, 2, 1), (26, 0, 2, 14, 2, 0), (27, 1, 0, 6, 2, 3), (27, 0, 12, 13, 6, 6), (30, 0, 12, 14, 3, 2),
+    (31, 0, 2, 6, 1, 1), (31, 0, 2, 14, 1, 0), (31, 0, 2, 3, 6, 6), (32, 0, 8, 10, 0, 2), (33, 1, 7, 5, 1, 3), (34, 0, 8, 9, 6, 6),
+    (35, 0, 12, 8, 5, 0), (35, 0, 12, 13, 7, 6), (38, 0, 4, 8, 4, 1), (38, 0, 4, 5, 7, 6), (43, 0, 2, 6, 5, 1), (43, 0, 2, 14, 5, 0),
+    (44, 0, 14, 10, 1, 0), (47, 1, 0, 2, 1, 4), (48, 0, 2, 14, 4, 0), (48, 0, 2, 6, 4, 1), (49, 1, 0, 6, 3, 3), (50, 0, 6, 10, 2, 1),
+    (50, 0, 6, 7, 6, 6), (53, 1, 1, 3, 3, 4), (53, 1, 1, 7, 3, 3), (55, 0, 8, 10, 3, 2), (55, 0, 8, 9, 7, 6), (58, 0, 2, 3, 7, 6),
+    (59, 0, 14, 15, 6, 6), (63, 0, 14, 10, 5, 0), (71, 0, 6, 10, 4, 1), (71, 0, 6, 7, 7, 6), (72, 1, 3, 5, 3, 4), (75, 0, 14, 15, 7, 6),
+    (78, 0, 10, 11, 6, 6), (83, 0, 10, 11, 7, 6),
 )
 TARGETS = ("y+", "y-", "zl", "x+", "x-", "zh", "sib")
 
@@ -64,6 +64,27 @@
 NOTHING = 127
 OWN = 10
 WHEN_A, WHEN_B, TRIGGERS = make_plan()
+
+
+def partners(n):
+    code = TRIGGERS[n]
+    if code == NOTHING:
+        return ()
+    half = code % 2
+    there = [WHEN_B[at * 2 + half] <= n if code < 32 else WHEN_A[at * 2 + half] < n for at in range(16)]
+    return there if any(there) else ()
+
+
+def make_groups():
+    groups = [[]]
+    for n in range(1, len(ORDER) + 1):
+        groups[-1].append(n)
+        if partners(n) and n < len(ORDER):
+            groups.append([])
+    return groups
+
+
+GROUPS = make_groups()
 LENGTHS = [(B_PIECES if copy[1] else A_PIECES)[copy[4]][1] for copy in COPIES]
 SENT = [sorted(range(len(COPIES)), key=lambda i: (LENGTHS[i], i)).index(n) for n in range(len(COPIES))]
 
@@ -238,29 +259,28 @@
         no_row = [meta_a[g, 32 + half * 2 + kk] for kk in range(2)]
         no_col = [meta_b[p, 96 + h * 4 + half * 2 + kk] for kk in range(2)]
         for kk in range(2):
-            for r in range(8):
+            at = h * 12 + half * 6 + kk * 3
+            for c in range(4):
+                low = b_all[qb, at + min(c, 2)]
+                high = b_all[qb, at + max(c - 1, 0)]
+                dense[kk * W:(kk + 1) * W, c * W:(c + 1) * W] = jnp.where(
+                    c == no_col[kk], jnp.zeros_like(low), jnp.where(c < no_col[kk], low, high))
+        for r in range(8):
+            left, right = [], []
+            for kk in range(2):
                 low = a_all[qa, first + kk * 7 + min(r, 6)]
                 high = a_all[qa, first + kk * 7 + max(r - 1, 0)]
-                dense[r * W:(r + 1) * W, kk * W:(kk + 1) * W] = jnp.where(
-                    r == no_row[kk], jnp.zeros_like(low), jnp.where(r < no_row[kk], low, high))
-        for c in range(4):
-            right = []
-            for kk in range(2):
-                at = h * 12 + half * 6 + kk * 3
-                low = b_all[qb, at + min(c, 2)]
-                high = b_all[qb, at + max(c - 1, 0)]
-                right.append(jnp.where(
-                    c == no_col[kk], jnp.zeros_like(low), jnp.where(c < no_col[kk], low, high)))
-            rows = []
-            for r in range(8):
+                left.append(jnp.where(
+                    r == no_row[kk], jnp.zeros_like(low), jnp.where(r < no_row[kk], low, high)))
                 cells = []
-                for kk in range(2):
+                for c in range(4):
                     passed = screen[own_rows[kk][r], own_cols[kk][c], half * 2 + kk, s].astype(F32)
-                    cells.append(dense[r * W:(r + 1) * W, kk * W:(kk + 1) * W] * passed.astype(BF16))
-                rows.append(jnp.concatenate(cells, axis=1))
-            left = jnp.concatenate(rows, axis=0)
-            part = jnp.dot(left, jnp.concatenate(right, axis=0), preferred_element_type=F32)
-            total[c * 8:(c + 1) * 8] += part.reshape(8, W, W)
+                    cells.append(dense[kk * W:(kk + 1) * W, c * W:(c + 1) * W] * passed.astype(BF16))
+                right.append(jnp.concatenate(cells, axis=1))
+            part = jnp.dot(
+                jnp.concatenate(left, axis=1), jnp.concatenate(right, axis=0), preferred_element_type=F32)
+            for c in range(4):
+                total[c * 8 + r] += part[:, c * W:(c + 1) * W]
 
     def pair_of(s):
         g, e = (col + s) & 15, (row + s) & 15
@@ -271,22 +291,16 @@
 
     def ready_after(n):
         code = TRIGGERS[n]
-        if code == NOTHING:
-            return I32(-1)
-        half, which = code % 2, code // 2 % 16
+        half, which, there = code % 2, code // 2 % 16, partners(n)
         if code < 32:
             g = 4 * ((y + which // 4) & 3) + 2 * (zl ^ (which // 2 % 2)) + (core ^ (which % 2))
             s = (g - col) & 15
             _, _, h, _, qb = pair_of(s)
-            there = [WHEN_B[at * 2 + half] <= n for at in range(16)]
             at = 2 * qb + h
         else:
             p = 2 * ((x + which // 4) & 3) + (zh ^ (which // 2 % 2))
             s = (p + 8 * (which % 2) - row) & 15
             at = pair_of(s)[3]
-            there = [WHEN_A[at * 2 + half] < n for at in range(16)]
-        if not any(there):
-            return I32(-1)
         both = lax.shift_right_logical(I32(sum(1 << i for i, v in enumerate(there) if v)), at) & 1
         return jnp.where(both == 1, 2 * s + half, -1)
 
@@ -294,15 +308,16 @@
         if high - low > 1:
             middle = (low + high) // 2
             return lax.cond(n < middle, lambda: receive(n, low, middle), lambda: receive(n, middle, high))
-        arrival_of(*ORDER[low - 1]).wait_recv()
-        for number, copy in enumerate(COPIES):
-            if copy[0] == low:
-                copy_of(number).start()
-        return ready_after(low)
-
-    @pl.loop(1, len(ORDER) + 1)
+        for arrival in GROUPS[low]:
+            arrival_of(*ORDER[arrival - 1]).wait_recv()
+            for number, copy in enumerate(COPIES):
+                if copy[0] == arrival:
+                    copy_of(number).start()
+        return ready_after(arrival) if partners(arrival) else I32(-1)
+
+    @pl.loop(0, len(GROUPS))
     def _(n):
-        code = receive(n, 1, len(ORDER) + 1)
+        code = receive(n, 0, len(GROUPS))
 
         @pl.when(code >= 0)
         def _():
@@ -386,7 +401,7 @@
             pltpu.VMEM((16, 28, W, W), BF16),
             pltpu.VMEM((8, 24, W, W), BF16),
             pltpu.VMEM((32, W, W), F32),
-            pltpu.VMEM((8 * W, 2 * W), BF16),
+            pltpu.VMEM((2 * W, 4 * W), BF16),
             pltpu.VMEM((16, 2, W, W), BF16),
             pltpu.SMEM((W,), I32),
             pltpu.SMEM((16, W), I32),

time: 87.1 us -> 86 us (0.987)
  Pallas kernels: 84.6 us -> 83.5 us
    pallas_call x1, Pallas kernels: 84.6 us -> 83.5 us  [on_device(): pl.pallas_call(kernel, out_shape=jax.ShapeDtypeStruct((16, 2, W, W), BF16...]
where the time goes in v5:
time: 86 us; the launch traced here: 85.9 us
  Pallas kernels  83.5 us (97%)
  local copies, waits for them, and re-layouts  2.31 us (3%)
    pallas_call x1, Pallas kernels, on_device(): pl.pallas_call(kernel, out_shape=jax.ShapeDtypeStruct((16, 2, W, W), BF16...  83.5 us
    unnamed x1, local copies, waits for them, and re-layouts  2.31 us

profile of v5, /device:TPU:1, one launch (start us, length us, event | category | flops | bytes accessed | tf_op | source)
XLA Modules:
  0.0 85.9 jit_solution(724703694046296123)
XLA Ops:
  0.0 83.5 %gather_multiply_send.1 = bf16[16,2,128,128]{3,2,1,0:T(8,128)(2,1)} custom-call(bf16[4,7,128,128]{3,2,1,0:T(8,128)(2,1)} %bitcast.13, bf16[8,3,128,128]{3,2,1,0:T(8,128)(2,1)} %bitcast.14, s32[4,7]{1,0:T(4,128)} %bitcast.17, s32[3,2,4]{2,1,0:T(2,128)} %bitcast.16, s32[7,3,4,16]{3,2,1,0:T(4,128)} %bitcast.15, s32[32]{0:T(128)} %bitcast.18, s32[32]{0:T(128)} %bitcast.19), custom_call_target="tpu_custom_call" | custom-call | flops 8600000512 | bytes 4000000 | tf_op jit(solution)/shard_map/gather_multiply_send/pallas_call | solution.py:388
  83.6 2.3 %copy.9 = bf16[1,1,16,2,128,128]{5,4,3,2,1,0:T(8,128)(2,1)} copy(bf16[1,1,16,2,128,128]{5,4,3,2,1,0:T(8,128)(2,1)} %bitcast.12) | data formatting | bytes 2097152

commit v6 on v5

--- a/solution.py
+++ b/solution.py
@@ -107,11 +107,11 @@
 
     barrier = pltpu.get_barrier_semaphore()
 
-    @pl.loop(1, 16)
+    @pl.loop(1, 16, unroll=15)
     def _(t):
         pl.semaphore_signal(barrier, inc=1, device_id=(row, rem(col + t, 16)), device_id_type=MESH)
 
-    @pl.loop(1, 8)
+    @pl.loop(1, 8, unroll=7)
     def _(t):
         pl.semaphore_signal(barrier, inc=1, device_id=(rem(row + t, 8), col), device_id_type=MESH)
 
@@ -201,11 +201,11 @@
     pl.semaphore_wait(barrier, 22)
     own = [(number, copy) for number, copy in enumerate(COPIES) if copy[0] == 0]
     first = [number for number, copy in own if in_half(copy) == 0]
-    @pl.loop(1, 16)
+    @pl.loop(1, 16, unroll=15)
     def _(t):
         meta_a_copy(t).start()
 
-    @pl.loop(1, 8)
+    @pl.loop(1, 8, unroll=7)
     def _(t):
         meta_b_copy(t).start()
 
@@ -337,7 +337,7 @@
     def own_copy():
         return pltpu.make_async_copy(stage.at[OWN], out.at[col], own_sem)
 
-    @pl.loop(0, 16)
+    @pl.loop(0, 16, unroll=4)
     def _(u):
         o = owner_at(u)
         for slot in range(2):

time: 86 us -> 85.9 us (level)
  no operation moved by 1% of the time
where the time goes in v6:
time: 85.9 us; the launch traced here: 85.8 us
  Pallas kernels  83.5 us (97%)
  local copies, waits for them, and re-layouts  2.31 us (3%)
    pallas_call x1, Pallas kernels, on_device(): pl.pallas_call(kernel, out_shape=jax.ShapeDtypeStruct((16, 2, W, W), BF16...  83.5 us
    unnamed x1, local copies, waits for them, and re-layouts  2.31 us

profile of v6, /device:TPU:1, one launch (start us, length us, event | category | flops | bytes accessed | tf_op | source)
XLA Modules:
  0.0 85.8 jit_solution(18207919539583547536)
XLA Ops:
  0.0 83.5 %gather_multiply_send.1 = bf16[16,2,128,128]{3,2,1,0:T(8,128)(2,1)} custom-call(bf16[4,7,128,128]{3,2,1,0:T(8,128)(2,1)} %bitcast.13, bf16[8,3,128,128]{3,2,1,0:T(8,128)(2,1)} %bitcast.14, s32[4,7]{1,0:T(4,128)} %bitcast.17, s32[3,2,4]{2,1,0:T(2,128)} %bitcast.16, s32[7,3,4,16]{3,2,1,0:T(4,128)} %bitcast.15, s32[32]{0:T(128)} %bitcast.18, s32[32]{0:T(128)} %bitcast.19), custom_call_target="tpu_custom_call" | custom-call | flops 8600000512 | bytes 4000000 | tf_op jit(solution)/shard_map/gather_multiply_send/pallas_call | solution.py:388
  83.5 2.3 %copy.9 = bf16[1,1,16,2,128,128]{5,4,3,2,1,0:T(8,128)(2,1)} copy(bf16[1,1,16,2,128,128]{5,4,3,2,1,0:T(8,128)(2,1)} %bitcast.12) | data formatting | bytes 2097152

commit v7 on v6

--- a/solution.py
+++ b/solution.py
@@ -11,36 +11,36 @@
 BF16, F32, I32 = jnp.bfloat16, jnp.float32, jnp.int32
 W = 128
 
-A_PIECES = ((0, 3), (3, 5), (8, 6), (14, 3), (17, 5), (22, 6), (0, 14), (14, 14))
+A_PIECES = ((0, 4), (4, 5), (9, 5), (14, 3), (17, 5), (22, 6), (0, 14), (14, 14))
 B_PIECES = ((0, 6), (6, 6), (12, 6), (18, 6))
 A_HALF = tuple(lo // 14 for lo, _ in A_PIECES)
 ORDER = (
-    (0, 4, 0), (1, 1, 2), (1, 2, 3), (0, 12, 1), (1, 2, 2), (1, 6, 1), (0, 4, 1), (1, 1, 0), (1, 2, 0), (0, 12, 4),
-    (0, 4, 2), (1, 4, 1), (1, 7, 2), (0, 6, 0), (0, 1, 7), (1, 1, 1), (1, 3, 2), (0, 12, 0), (0, 5, 6), (0, 2, 0),
-    (0, 4, 3), (1, 6, 0), (1, 7, 0), (0, 4, 5), (0, 8, 1), (0, 2, 2), (0, 12, 2), (0, 1, 6), (1, 4, 3), (0, 12, 3),
-    (0, 2, 1), (0, 8, 0), (1, 7, 1), (0, 8, 2), (0, 12, 5), (1, 4, 2), (0, 3, 6), (0, 4, 4), (1, 3, 0), (0, 9, 6),
-    (1, 4, 0), (0, 13, 6), (0, 2, 5), (0, 14, 1), (0, 5, 7), (0, 6, 1), (0, 14, 2), (0, 2, 4), (0, 13, 7), (0, 6, 2),
-    (1, 5, 0), (0, 8, 4), (1, 1, 3), (0, 8, 5), (0, 8, 3), (1, 5, 2), (0, 7, 6), (0, 2, 3), (0, 14, 0), (1, 3, 1),
-    (1, 6, 2), (1, 2, 1), (0, 14, 5), (0, 6, 5), (0, 3, 7), (1, 5, 1), (0, 9, 7), (0, 14, 3), (0, 15, 6), (0, 6, 3),
-    (0, 6, 4), (1, 3, 3), (1, 6, 3), (0, 10, 0), (0, 14, 4), (0, 10, 2), (0, 7, 7), (0, 10, 1), (1, 7, 3), (0, 15, 7),
-    (0, 10, 3), (0, 10, 5), (0, 10, 4), (0, 11, 6), (1, 5, 3), (0, 11, 7),
+    (0, 1, 7), (0, 1, 6), (0, 2, 0), (0, 4, 0), (1, 2, 0), (1, 6, 0), (1, 2, 3), (1, 6, 3), (0, 12, 4), (0, 12, 1),
+    (1, 1, 0), (0, 4, 1), (0, 12, 5), (1, 4, 0), (1, 6, 1), (0, 4, 5), (1, 2, 2), (0, 12, 0), (0, 12, 2), (0, 4, 3),
+    (1, 2, 1), (0, 4, 4), (0, 4, 2), (1, 7, 0), (1, 4, 3), (0, 2, 2), (0, 2, 1), (1, 1, 3), (0, 12, 3), (0, 3, 6),
+    (0, 5, 6), (0, 2, 4), (1, 4, 1), (0, 8, 3), (0, 8, 5), (0, 8, 4), (0, 13, 6), (1, 3, 0), (0, 5, 7), (1, 5, 0),
+    (0, 8, 0), (1, 1, 1), (0, 6, 0), (0, 8, 1), (1, 4, 2), (0, 14, 0), (0, 8, 2), (0, 14, 2), (1, 3, 3), (0, 9, 7),
+    (1, 7, 3), (0, 9, 6), (0, 2, 5), (0, 6, 1), (0, 14, 1), (1, 7, 1), (0, 2, 3), (0, 6, 2), (0, 14, 4), (1, 3, 1),
+    (0, 15, 6), (0, 3, 7), (0, 6, 4), (1, 6, 2), (1, 1, 2), (0, 7, 6), (0, 6, 3), (0, 6, 5), (1, 5, 3), (0, 13, 7),
+    (0, 14, 3), (0, 14, 5), (0, 7, 7), (0, 10, 1), (0, 10, 2), (1, 5, 1), (1, 3, 2), (0, 15, 7), (0, 10, 0), (0, 10, 3),
+    (0, 10, 4), (0, 10, 5), (1, 7, 2), (0, 11, 6), (0, 11, 7), (1, 5, 2),
 )
 COPIES = (
-    (0, 0, 0, 12, 1, 0), (0, 0, 0, 4, 0, 1), (0, 1, 0, 1, 2, 5), (0, 1, 0, 2, 2, 4), (0, 0, 0, 12, 0, 0), (0, 1, 0, 6, 1, 3),
-    (0, 1, 0, 2, 3, 4), (0, 0, 0, 4, 2, 1), (0, 0, 0, 12, 5, 0), (0, 0, 0, 1, 7, 6), (0, 0, 0, 4, 1, 1), (0, 0, 0, 4, 4, 1),
-    (0, 0, 0, 2, 0, 2), (0, 1, 0, 1, 0, 5), (1, 1, 0, 6, 0, 3), (1, 1, 0, 1, 1, 5), (1, 0, 0, 4, 5, 1), (1, 0, 4, 6, 0, 2),
-    (1, 1, 0, 2, 0, 4), (2, 1, 1, 7, 2, 3), (2, 1, 1, 3, 2, 4), (2, 0, 0, 12, 4, 0), (3, 0, 0, 1, 6, 6), (3, 0, 0, 12, 2, 0),
-    (3, 1, 2, 4, 3, 4), (4, 0, 12, 8, 1, 0), (4, 0, 0, 2, 2, 2), (4, 0, 0, 4, 3, 1), (5, 1, 2, 4, 2, 4), (6, 0, 0, 12, 3, 0),
-    (6, 1, 6, 4, 1, 3), (8, 1, 1, 3, 0, 4), (8, 1, 1, 7, 0, 3), (9, 0, 0, 2, 1, 2), (11, 0, 0, 2, 5, 2), (11, 0, 4, 8, 2, 1),
-    (11, 0, 4, 5, 6, 6), (12, 0, 0, 2, 4, 2), (14, 1, 0, 1, 3, 5), (16, 1, 1, 3, 1, 4), (16, 1, 1, 7, 1, 3), (17, 1, 3, 5, 2, 4),
-    (17, 0, 0, 2, 3, 2), (18, 0, 12, 14, 0, 2), (18, 0, 12, 8, 0, 0), (21, 0, 4, 6, 3, 2), (21, 0, 4, 8, 3, 1), (22, 1, 6, 4, 0, 3),
-    (23, 1, 7, 5, 0, 3), (26, 0, 2, 6, 2, 1), (26, 0, 2, 14, 2, 0), (27, 1, 0, 6, 2, 3), (27, 0, 12, 13, 6, 6), (30, 0, 12, 14, 3, 2),
-    (31, 0, 2, 6, 1, 1), (31, 0, 2, 14, 1, 0), (31, 0, 2, 3, 6, 6), (32, 0, 8, 10, 0, 2), (33, 1, 7, 5, 1, 3), (34, 0, 8, 9, 6, 6),
-    (35, 0, 12, 8, 5, 0), (35, 0, 12, 13, 7, 6), (38, 0, 4, 8, 4, 1), (38, 0, 4, 5, 7, 6), (43, 0, 2, 6, 5, 1), (43, 0, 2, 14, 5, 0),
-    (44, 0, 14, 10, 1, 0), (47, 1, 0, 2, 1, 4), (48, 0, 2, 14, 4, 0), (48, 0, 2, 6, 4, 1), (49, 1, 0, 6, 3, 3), (50, 0, 6, 10, 2, 1),
-    (50, 0, 6, 7, 6, 6), (53, 1, 1, 3, 3, 4), (53, 1, 1, 7, 3, 3), (55, 0, 8, 10, 3, 2), (55, 0, 8, 9, 7, 6), (58, 0, 2, 3, 7, 6),
-    (59, 0, 14, 15, 6, 6), (63, 0, 14, 10, 5, 0), (71, 0, 6, 10, 4, 1), (71, 0, 6, 7, 7, 6), (72, 1, 3, 5, 3, 4), (75, 0, 14, 15, 7, 6),
-    (78, 0, 10, 11, 6, 6), (83, 0, 10, 11, 7, 6),
+    (0, 0, 0, 2, 0, 2), (0, 1, 0, 6, 3, 3), (0, 0, 0, 4, 0, 1), (0, 1, 0, 1, 3, 5), (0, 0, 0, 12, 5, 0), (0, 1, 0, 2, 0, 4),
+    (0, 0, 0, 12, 0, 0), (0, 0, 0, 4, 3, 1), (0, 0, 0, 4, 2, 1), (0, 0, 0, 1, 7, 6), (0, 0, 0, 1, 6, 6), (0, 1, 0, 6, 0, 3),
+    (0, 0, 0, 4, 1, 1), (0, 0, 0, 12, 4, 0), (0, 1, 0, 6, 1, 3), (0, 1, 0, 2, 3, 4), (1, 1, 0, 2, 1, 4), (2, 1, 0, 1, 0, 5),
+    (2, 0, 0, 4, 5, 1), (3, 0, 0, 2, 2, 2), (4, 0, 4, 6, 0, 2), (4, 0, 0, 2, 1, 2), (5, 0, 0, 12, 1, 0), (5, 0, 0, 12, 2, 0),
+    (6, 1, 6, 4, 0, 3), (7, 1, 0, 2, 2, 4), (7, 1, 2, 4, 3, 4), (9, 0, 12, 8, 4, 0), (9, 0, 0, 12, 3, 0), (9, 0, 0, 2, 4, 2),
+    (10, 0, 0, 4, 4, 1), (10, 0, 12, 8, 1, 0), (11, 1, 1, 7, 0, 3), (11, 1, 1, 3, 0, 4), (15, 1, 6, 4, 1, 3), (15, 1, 0, 1, 1, 5),
+    (16, 0, 4, 8, 5, 1), (17, 1, 2, 4, 2, 4), (18, 0, 12, 8, 0, 0), (18, 0, 12, 14, 0, 2), (18, 0, 0, 2, 5, 2), (19, 0, 0, 2, 3, 2),
+    (19, 0, 12, 13, 6, 6), (20, 1, 0, 1, 2, 5), (20, 0, 4, 6, 3, 2), (20, 0, 4, 8, 3, 1), (22, 0, 4, 5, 7, 6), (23, 0, 4, 8, 2, 1),
+    (23, 0, 4, 5, 6, 6), (24, 1, 7, 5, 0, 3), (26, 0, 2, 14, 2, 0), (26, 0, 2, 6, 2, 1), (27, 0, 2, 6, 1, 1), (27, 0, 2, 14, 1, 0),
+    (27, 0, 2, 3, 6, 6), (28, 1, 1, 7, 3, 3), (28, 1, 1, 3, 3, 4), (29, 0, 12, 14, 3, 2), (29, 0, 12, 13, 7, 6), (32, 0, 2, 6, 4, 1),
+    (32, 0, 2, 14, 4, 0), (34, 0, 8, 10, 3, 2), (36, 0, 8, 9, 7, 6), (41, 0, 8, 10, 0, 2), (42, 1, 1, 7, 1, 3), (42, 1, 1, 3, 1, 4),
+    (43, 1, 0, 6, 2, 3), (47, 0, 8, 9, 6, 6), (49, 1, 3, 5, 3, 4), (53, 0, 2, 6, 5, 1), (53, 0, 2, 14, 5, 0), (55, 0, 14, 10, 1, 0),
+    (55, 0, 14, 15, 6, 6), (56, 1, 7, 5, 1, 3), (57, 0, 2, 3, 7, 6), (58, 0, 6, 10, 2, 1), (58, 0, 6, 7, 6, 6), (59, 0, 14, 10, 4, 0),
+    (65, 1, 1, 7, 2, 3), (65, 1, 1, 3, 2, 4), (68, 0, 6, 10, 5, 1), (68, 0, 6, 7, 7, 6), (72, 0, 14, 15, 7, 6), (77, 1, 3, 5, 2, 4),
+    (79, 0, 10, 11, 6, 6), (82, 0, 10, 11, 7, 6),
 )
 TARGETS = ("y+", "y-", "zl", "x+", "x-", "zh", "sib")
 
@@ -270,11 +270,11 @@
             for kk in range(2):
                 low = a_all[qa, first + kk * 7 + min(r, 6)]
                 high = a_all[qa, first + kk * 7 + max(r - 1, 0)]
-                left.append(jnp.where(
-                    r == no_row[kk], jnp.zeros_like(low), jnp.where(r < no_row[kk], low, high)))
+                left.append(jnp.where(r < no_row[kk], low, high))
                 cells = []
                 for c in range(4):
-                    passed = screen[own_rows[kk][r], own_cols[kk][c], half * 2 + kk, s].astype(F32)
+                    passed = screen[own_rows[kk][r], own_cols[kk][c], half * 2 + kk, s]
+                    passed = jnp.where(r == no_row[kk], 0, passed).astype(F32)
                     cells.append(dense[kk * W:(kk + 1) * W, c * W:(c + 1) * W] * passed.astype(BF16))
                 right.append(jnp.concatenate(cells, axis=1))
             part = jnp.dot(

time: 85.9 us -> 85.7 us (level)
  no operation moved by 1% of the time
where the time goes in v7:
time: 85.7 us; the launch traced here: 85.5 us
  Pallas kernels  83.2 us (97%)
  local copies, waits for them, and re-layouts  2.31 us (3%)
    pallas_call x1, Pallas kernels, on_device(): pl.pallas_call(kernel, out_shape=jax.ShapeDtypeStruct((16, 2, W, W), BF16...  83.2 us
    unnamed x1, local copies, waits for them, and re-layouts  2.31 us

profile of v7, /device:TPU:1, one launch (start us, length us, event | category | flops | bytes accessed | tf_op | source)
XLA Modules:
  0.0 85.5 jit_solution(1100238577543386422)
XLA Ops:
  0.0 83.2 %gather_multiply_send.1 = bf16[16,2,128,128]{3,2,1,0:T(8,128)(2,1)} custom-call(bf16[4,7,128,128]{3,2,1,0:T(8,128)(2,1)} %bitcast.13, bf16[8,3,128,128]{3,2,1,0:T(8,128)(2,1)} %bitcast.14, s32[4,7]{1,0:T(4,128)} %bitcast.17, s32[3,2,4]{2,1,0:T(2,128)} %bitcast.16, s32[7,3,4,16]{3,2,1,0:T(4,128)} %bitcast.15, s32[32]{0:T(128)} %bitcast.18, s32[32]{0:T(128)} %bitcast.19), custom_call_target="tpu_custom_call" | custom-call | flops 8600000512 | bytes 4000000 | tf_op jit(solution)/shard_map/gather_multiply_send/pallas_call | solution.py:388
  83.2 2.3 %copy.9 = bf16[1,1,16,2,128,128]{5,4,3,2,1,0:T(8,128)(2,1)} copy(bf16[1,1,16,2,128,128]{5,4,3,2,1,0:T(8,128)(2,1)} %bitcast.12) | data formatting | bytes 2097152
